TPU v7x, 32 devices: a whole 2x2x4 slice. The times are simulated.
32 devices in a mesh: dp: 8 (over y, x, core), tensor: 4 (over z).
Axes of the slice: x: 2, y: 2, z: 4, core: 2. Of those that a mesh axis runs over, the one named last changes fastest.
Arguments:
- tokens: bfloat16 [1024, 8, 1024], P('tensor', 'dp'), may hold values from -6 to 6
- cotangent: bfloat16 [1024, 8, 1024], P('tensor', 'dp'), may hold values from -6 to 6
- clip_mask: int32 [8], P('dp'), may hold values from 0 to 1, as said below
- positions: int32 [3, 8, 1024], P(None, 'dp'), may hold values from 0 to 15
- triple_weight: bfloat16 [2, 1024, 3, 1024], P(None, 'dp', None, 'tensor'), may hold values from -0.1875 to 0.1875
- triple_bias: bfloat16 [2, 3, 1024], P(None, None, 'tensor'), may hold values from -0.75 to 0.75
- exit_weight: bfloat16 [2, 1024, 1024], P(None, 'tensor', 'dp'), may hold values from -2 to 2
- expand_weight: bfloat16 [2, 1024, 4096], P(None, 'dp', 'tensor'), may hold values from -0.1875 to 0.1875
- expand_bias: bfloat16 [2, 4096], P(None, 'tensor'), may hold values from -4 to 4
- shrink_weight: bfloat16 [2, 4096, 1024], P(None, 'tensor', 'dp'), may hold values from -0.09375 to 0.09375
- norm_gain: bfloat16 [2, 2, 1024], replicated, may hold values from 0.5 to 1.5
- norm_shift: bfloat16 [2, 2, 1024], replicated, may hold values from -3 to 3
- branch_bias: bfloat16 [2, 2, 1024], replicated, may hold values from -4 to 4
Outputs:
- mixed: float32 [1024, 8, 1024], P('tensor', 'dp')
- tokens_gradient: float32 [1024, 8, 1024], P('tensor', 'dp')
- triple_gradient: float32 [2, 1024, 3, 1024], P(None, 'dp', None, 'tensor')
- triple_bias_gradient: float32 [2, 3, 1024], P(None, None, 'tensor')
- exit_gradient: float32 [2, 1024, 1024], P(None, 'tensor', 'dp')
- expand_gradient: float32 [2, 1024, 4096], P(None, 'dp', 'tensor')
- expand_bias_gradient: float32 [2, 4096], P(None, 'tensor')
- shrink_gradient: float32 [2, 4096, 1024], P(None, 'tensor', 'dp')
- gain_gradient: float32 [2, 2, 1024], replicated
- shift_gradient: float32 [2, 2, 1024], replicated
- branch_bias_gradient: float32 [2, 2, 1024], replicated
Inputs may be any that keep to these rules, and one draw needn't show every extreme that they name: `clip_mask`: exactly 1 of the 8 slots hold 0.
All inputs are finite; a program needn't handle non-finite values.
Results may differ from a plain program's by a relative error of at most 0.015.
Values may be sent and summed in bfloat16 or wider, within the bound.
A program may use at most 128 MiB of HBM per device.

v0:
```python
import jax
import jax.numpy as jnp
from jax import lax
from jax.sharding import PartitionSpec as P

HEAD_DIM = 64
ROT = 20
LAYERS = 2
SEQ = 1024
QBLOCK = 512


EPSILON = 1e-06
SQRT_HALF = 0.7071067811865476
ROOT_TWO_PI = 2.5066282746310002


def rotary_tables(positions):
    halfway = ROT // 2
    indices = jnp.arange(halfway, dtype=jnp.float32)
    frequency = 10000.0 ** (-indices / halfway)
    angles = jnp.transpose(positions.astype(jnp.float32), (0, 2, 1))[..., None] * frequency
    return (jnp.cos(angles)[:, :, :, None, :], jnp.sin(angles)[:, :, :, None, :])


def rotate(values, cosines, sines):
    halfway = ROT // 2
    pieces = []
    for coord_index in range(3):
        offset = coord_index * ROT
        former = values[..., offset : offset + halfway]
        latter = values[..., offset + halfway : offset + ROT]
        pieces.append(former * cosines[coord_index] - latter * sines[coord_index])
        pieces.append(latter * cosines[coord_index] + former * sines[coord_index])
    pieces.append(values[..., 3 * ROT :])
    return jnp.concatenate(pieces, axis=-1)


def normalize(values, gain_row, shift_row):
    center = values - jnp.mean(values, axis=-1, keepdims=True)
    inverse = lax.rsqrt(jnp.mean(center * center, axis=-1, keepdims=True) + EPSILON)
    scaled = center * inverse
    return (scaled * gain_row + shift_row, scaled, inverse)


def norm_back(upstream, scaled, inverse, gain_row):
    weighted = upstream * gain_row
    first_mean = jnp.mean(weighted, axis=-1, keepdims=True)
    second_mean = jnp.mean(weighted * scaled, axis=-1, keepdims=True)
    return inverse * (weighted - first_mean - scaled * second_mean)


def gelu_slope(inner_sum):
    return (
        0.5 * (1.0 + lax.erf(inner_sum * SQRT_HALF))
        + inner_sum * jnp.exp(-0.5 * inner_sum * inner_sum) / ROOT_TWO_PI
    )


def to_items(array):
    seq_length, clip_count, head_count, head_width = array.shape
    return jnp.transpose(array, (1, 2, 0, 3)).reshape(
        clip_count * head_count, seq_length, head_width
    )


def from_items(array, clip_count):
    item_count, seq_length, head_width = array.shape
    return jnp.transpose(
        array.reshape(clip_count, item_count // clip_count, seq_length, head_width), (2, 0, 1, 3)
    )


def attend(queries, key_items, values):
    factor = HEAD_DIM ** (-0.5)
    block_count = SEQ // QBLOCK

    def one_item(triple):
        query_rows, key_rows, value_rows = triple

        def one_block(query_block):
            scores = (
                jnp.einsum("qe,ke->qk", query_block, key_rows, preferred_element_type=jnp.float32)
                * factor
            )
            highest = jnp.max(scores, axis=-1, keepdims=True)
            weights = jnp.exp(scores - highest)
            summed = jnp.sum(weights, axis=-1, keepdims=True)
            chances = (weights / summed).astype(jnp.bfloat16)
            output = jnp.einsum(
                "qk,ke->qe", chances, value_rows, preferred_element_type=jnp.float32
            )
            return (output.astype(jnp.bfloat16), (highest + jnp.log(summed))[:, 0])

        outputs, logsums = lax.map(one_block, query_rows.reshape(block_count, QBLOCK, HEAD_DIM))
        return (outputs.reshape(SEQ, HEAD_DIM), logsums.reshape(SEQ))

    return lax.map(one_item, (queries, key_items, values))


def attend_back(queries, key_items, values, out_grads, logsums):
    factor = HEAD_DIM ** (-0.5)
    block_count = SEQ // QBLOCK

    def one_item(group):
        query_rows, key_rows, value_rows, grad_rows, logsum_rows = group

        def one_block(carry, blocked):
            key_total, value_total = carry
            query_block, grad_block, logsum_block = blocked
            scores = (
                jnp.einsum("qe,ke->qk", query_block, key_rows, preferred_element_type=jnp.float32)
                * factor
            )
            chances = jnp.exp(scores - logsum_block[:, None])
            value_total = value_total + jnp.einsum(
                "qk,qe->ke",
                chances.astype(jnp.bfloat16),
                grad_block,
                preferred_element_type=jnp.float32,
            )
            chance_grad = jnp.einsum(
                "qe,ke->qk", grad_block, value_rows, preferred_element_type=jnp.float32
            )
            center = jnp.sum(chances * chance_grad, axis=-1, keepdims=True)
            score_grad = (chances * (chance_grad - center)).astype(jnp.bfloat16)
            query_grad = (
                jnp.einsum("qk,ke->qe", score_grad, key_rows, preferred_element_type=jnp.float32)
                * factor
            )
            key_total = (
                key_total
                + jnp.einsum(
                    "qk,qe->ke", score_grad, query_block, preferred_element_type=jnp.float32
                )
                * factor
            )
            return ((key_total, value_total), query_grad)

        zeros = jnp.zeros((SEQ, HEAD_DIM), jnp.float32)
        blocked_rows = (
            query_rows.reshape(block_count, QBLOCK, HEAD_DIM),
            grad_rows.reshape(block_count, QBLOCK, HEAD_DIM),
            logsum_rows.reshape(block_count, QBLOCK),
        )
        (key_total, value_total), query_grads = lax.scan(one_block, (zeros, zeros), blocked_rows)
        return (query_grads.reshape(SEQ, HEAD_DIM), key_total, value_total)

    return lax.map(one_item, (queries, key_items, values, out_grads, logsums))


def shards(
    tokens,
    cotangent,
    clip_mask,
    positions,
    triple_weight,
    triple_bias,
    exit_weight,
    expand_weight,
    expand_bias,
    shrink_weight,
    norm_gain,
    norm_shift,
    branch_bias,
):
    row_count = tokens.shape[0]
    clip_count = tokens.shape[1]
    local_width = triple_weight.shape[3]
    head_count = local_width // HEAD_DIM
    cosines, sines = rotary_tables(positions)
    live = clip_mask.astype(jnp.float32)[None, :, None]

    def spread_rows(normed):
        return lax.all_gather(normed, "tensor", axis=0, tiled=True)

    def spread_grads(upstream_low):
        return lax.all_gather(upstream_low, "tensor", axis=0, tiled=True)

    def collect_rows(operand, matrix, pattern):

        def partial_term(offset, row_span):
            return jnp.einsum(pattern, operand, matrix, preferred_element_type=jnp.float32)

        return lax.psum_scatter(
            partial_term(jnp.int32(0), row_count * lax.axis_size("tensor")).astype(jnp.bfloat16),
            "tensor",
            scatter_dimension=0,
            tiled=True,
        ).astype(jnp.float32)

    def collect_grads(operand, matrix, pattern):

        def partial_term(offset, row_span):
            return jnp.einsum(pattern, operand, matrix, preferred_element_type=jnp.float32)

        return lax.psum_scatter(
            partial_term(jnp.int32(0), row_count * lax.axis_size("tensor")).astype(jnp.bfloat16),
            "tensor",
            scatter_dimension=0,
            tiled=True,
        ).astype(jnp.float32)

    hidden = tokens.astype(jnp.float32)
    saved = []
    for layer_index in range(LAYERS):
        fetched = (
            lax.all_gather(triple_weight[layer_index], "dp", axis=0, tiled=True),
            lax.all_gather(exit_weight[layer_index], "dp", axis=1, tiled=True),
            lax.all_gather(expand_weight[layer_index], "dp", axis=0, tiled=True),
            lax.all_gather(shrink_weight[layer_index], "dp", axis=1, tiled=True),
        )
        triple_full, exit_full, expand_full, shrink_full = fetched
        gain_pair = norm_gain[layer_index].astype(jnp.float32)
        shift_pair = norm_shift[layer_index].astype(jnp.float32)
        bias_pair = branch_bias[layer_index].astype(jnp.float32)
        normed, scaled_one, inverse_one = normalize(hidden, gain_pair[0], shift_pair[0])
        gathered_one = spread_rows(normed.astype(jnp.bfloat16))
        mixed_triple = jnp.einsum(
            "scd,dtf->sctf", gathered_one, triple_full, preferred_element_type=jnp.float32
        ) + triple_bias[layer_index].astype(jnp.float32)
        split_heads = mixed_triple.reshape(SEQ, clip_count, 3, head_count, HEAD_DIM)
        query_items = to_items(rotate(split_heads[:, :, 0], cosines, sines).astype(jnp.bfloat16))
        key_items = to_items(rotate(split_heads[:, :, 1], cosines, sines).astype(jnp.bfloat16))
        value_items = to_items(split_heads[:, :, 2].astype(jnp.bfloat16))
        attended_items, logsums = attend(query_items, key_items, value_items)
        attended = from_items(attended_items, clip_count).reshape(SEQ, clip_count, local_width)
        hidden = hidden + (collect_rows(attended, exit_full, "sce,ed->scd") + bias_pair[0])
        normed, scaled_two, inverse_two = normalize(hidden, gain_pair[1], shift_pair[1])
        gathered_two = spread_rows(normed.astype(jnp.bfloat16))
        inner_sum = jnp.einsum(
            "scd,df->scf", gathered_two, expand_full, preferred_element_type=jnp.float32
        ) + expand_bias[layer_index].astype(jnp.float32)
        activated = jax.nn.gelu(inner_sum, approximate=False).astype(jnp.bfloat16)
        hidden = hidden + (collect_rows(activated, shrink_full, "scf,fd->scd") + bias_pair[1])
        saved.append(
            (
                gathered_one,
                scaled_one,
                inverse_one,
                query_items,
                key_items,
                value_items,
                logsums,
                attended,
                scaled_two,
                inverse_two,
                gathered_two,
                inner_sum,
                activated,
                fetched,
            )
        )
    mixed = hidden * live
    upstream = cotangent.astype(jnp.float32) * live
    collected = [None] * LAYERS
    gain_parts = [None] * LAYERS
    shift_parts = [None] * LAYERS
    bias_parts = [None] * LAYERS
    triple_bias_parts = [None] * LAYERS
    expand_bias_parts = [None] * LAYERS
    for layer_index in reversed(range(LAYERS)):
        (
            gathered_one,
            scaled_one,
            inverse_one,
            query_items,
            key_items,
            value_items,
            logsums,
            attended,
            scaled_two,
            inverse_two,
            gathered_two,
            inner_sum,
            activated,
            fetched,
        ) = saved[layer_index]
        triple_full, exit_full, expand_full, shrink_full = (
            lax.all_gather(triple_weight[layer_index], "dp", axis=0, tiled=True),
            lax.all_gather(exit_weight[layer_index], "dp", axis=1, tiled=True),
            lax.all_gather(expand_weight[layer_index], "dp", axis=0, tiled=True),
            lax.all_gather(shrink_weight[layer_index], "dp", axis=1, tiled=True),
        )
        gain_pair = norm_gain[layer_index].astype(jnp.float32)
        shrink_low = upstream.astype(jnp.bfloat16)
        bias_two = jnp.sum(shrink_low, axis=(0, 1), dtype=jnp.float32)
        full_grad = spread_grads(shrink_low)
        shrink_grad = jnp.einsum(
            "scf,scd->fd", activated, full_grad, preferred_element_type=jnp.float32
        )
        active_grad = jnp.einsum(
            "scd,fd->scf", full_grad, shrink_full, preferred_element_type=jnp.float32
        )
        inner_low = (active_grad * gelu_slope(inner_sum)).astype(jnp.bfloat16)
        expand_bias_parts[layer_index] = jnp.sum(inner_low, axis=(0, 1), dtype=jnp.float32)
        expand_grad = jnp.einsum(
            "scd,scf->df", gathered_two, inner_low, preferred_element_type=jnp.float32
        )
        normed_grad = collect_grads(inner_low, expand_full, "scf,df->scd")
        gain_two = jnp.sum(normed_grad * scaled_two, axis=(0, 1))
        shift_two = jnp.sum(normed_grad, axis=(0, 1))
        upstream = upstream + norm_back(normed_grad, scaled_two, inverse_two, gain_pair[1])
        branch_low = upstream.astype(jnp.bfloat16)
        bias_one = jnp.sum(branch_low, axis=(0, 1), dtype=jnp.float32)
        full_grad = spread_grads(branch_low)
        exit_grad = jnp.einsum(
            "sce,scd->ed", attended, full_grad, preferred_element_type=jnp.float32
        )
        attended_grad = jnp.einsum(
            "scd,ed->sce", full_grad, exit_full, preferred_element_type=jnp.float32
        ).astype(jnp.bfloat16)
        grad_items = to_items(attended_grad.reshape(SEQ, clip_count, head_count, HEAD_DIM))
        query_grad, key_grad, value_grad = attend_back(
            query_items, key_items, value_items, grad_items, logsums
        )
        query_back = rotate(from_items(query_grad, clip_count), cosines, -sines)
        key_back = rotate(from_items(key_grad, clip_count), cosines, -sines)
        value_back = from_items(value_grad, clip_count)
        triple_low = (
            jnp.stack([query_back, key_back, value_back], axis=2)
            .reshape(SEQ, clip_count, 3, local_width)
            .astype(jnp.bfloat16)
        )
        triple_bias_parts[layer_index] = jnp.sum(triple_low, axis=(0, 1), dtype=jnp.float32)
        triple_grad = jnp.einsum(
            "scd,sctf->dtf", gathered_one, triple_low, preferred_element_type=jnp.float32
        )
        normed_grad = collect_grads(triple_low, triple_full, "sctf,dtf->scd")
        gain_one = jnp.sum(normed_grad * scaled_one, axis=(0, 1))
        shift_one = jnp.sum(normed_grad, axis=(0, 1))
        upstream = upstream + norm_back(normed_grad, scaled_one, inverse_one, gain_pair[0])
        gain_parts[layer_index] = jnp.stack([gain_one, gain_two])
        shift_parts[layer_index] = jnp.stack([shift_one, shift_two])
        bias_parts[layer_index] = jnp.stack([bias_one, bias_two])
        collected[layer_index] = (
            lax.psum_scatter(triple_grad, "dp", scatter_dimension=0, tiled=True),
            lax.psum_scatter(exit_grad, "dp", scatter_dimension=1, tiled=True),
            lax.psum_scatter(expand_grad, "dp", scatter_dimension=0, tiled=True),
            lax.psum_scatter(shrink_grad, "dp", scatter_dimension=1, tiled=True),
        )
    stacked = [
        jnp.stack([collected[layer_index][member] for layer_index in range(LAYERS)])
        for member in range(4)
    ]
    triple_total, exit_total, expand_total, shrink_total = stacked
    gain_total, shift_total, bias_total = lax.psum(
        (jnp.stack(gain_parts), jnp.stack(shift_parts), jnp.stack(bias_parts)), ("dp", "tensor")
    )
    triple_bias_total, expand_bias_total = lax.psum(
        (jnp.stack(triple_bias_parts), jnp.stack(expand_bias_parts)), "dp"
    )
    return (
        mixed,
        upstream,
        triple_total,
        triple_bias_total,
        exit_total,
        expand_total,
        expand_bias_total,
        shrink_total,
        gain_total,
        shift_total,
        bias_total,
    )


def solution(mesh):
    return jax.shard_map(
        shards,
        mesh=mesh,
        in_specs=(
            P("tensor", "dp", None),
            P("tensor", "dp", None),
            P("dp"),
            P(None, "dp", None),
            P(None, "dp", None, "tensor"),
            P(None, None, "tensor"),
            P(None, "tensor", "dp"),
            P(None, "dp", "tensor"),
            P(None, "tensor"),
            P(None, "tensor", "dp"),
            P(),
            P(),
            P(),
        ),
        out_specs=(
            P("tensor", "dp", None),
            P("tensor", "dp", None),
            P(None, "dp", None, "tensor"),
            P(None, None, "tensor"),
            P(None, "tensor", "dp"),
            P(None, "dp", "tensor"),
            P(None, "tensor"),
            P(None, "tensor", "dp"),
            P(),
            P(),
            P(),
        ),
        check_vma=False,
    )
```

profile of v0, /device:TPU:1, one launch (start us, length us, event | category | flops | bytes accessed | tf_op | source)
XLA Modules:
  0.0 1528.5 jit_solution(13057020448451312139)
XLA Ops:
  18.6 12.9 all-gather.1
  32.3 7.2 all-gather.39.cloned.1.call-done
  39.5 47.7 %all-gather.23.cloned.1.call-done = bf16[1024,1,1024]{2,0,1:T(8,128)(2,1)} async-done(((bf16[256,1,1024]{2,0,1:T(8,128)(2,1)}), bf16[1024,1,1024]{2,0,1:T(8,128)(2,1)}) %all-gather.23.cloned.1.call-update) | async-done | bytes 2097168 | tf_op jit(solution)/shard_map/all_gather | solution.py:175
  87.2 3.9 fusion.132
  93.9 12.1 concatenate.87
  110.3 28.1 %while.107 = (s32[]{:T(128)}, bf16[4,1024,64]{1,2,0:T(8,128)(2,1)}, f32[4,1024]{1,0:T(4,128)}, bf16[4,1024,64]{2,1,0:T(8,128)(2,1)S(1)}, bf16[4,1024,64]{2,1,0:T...) while((s32[]{:T(128)}, bf16[4,1024,64]{1,2,0:T(8,128)(2,1)}, ...), condition=%wide.region_7.8_spmd, body=%wide.region_2.7_spmd.sunk | while | flops 138968576 | bytes 8622382 | solution.py:98
  138.3 4.0 convert_bitcast_fusion.5
  145.0 40.0 %reduce-scatter.17.cloned.1.call-done = bf16[256,1,1024]{2,0,1:T(8,128)(2,1)} async-done(((bf16[1024,1,1024]{2,0,1:T(8,128)(2,1)}), bf16[256,1,1024]{2,0,1:T(8,128)(2,1)}) %reduce-scatter.17.cloned.1.call-update) | async-done | bytes 524304 | tf_op jit(solution)/shard_map/reduce_scatter | solution.py:185
  192.6 22.7 %all-gather.41.cloned.1.call-done = bf16[1,1024,1024]{2,1,0:T(8,128)(2,1)} async-done(((bf16[1,128,1024]{2,1,0:T(8,128)(2,1)}), bf16[1,1024,1024]{2,1,0:T(8,128)(2,1)}) %all-gather.41.cloned.1.call-update) | async-done | bytes 2097168 | tf_op jit(solution)/shard_map/all_gather | solution.py:210
  215.3 47.6 %all-gather.25.cloned.1.call-done = bf16[1024,1,1024]{2,0,1:T(8,128)(2,1)} async-done(((bf16[256,1,1024]{2,0,1:T(8,128)(2,1)}), bf16[1024,1,1024]{2,0,1:T(8,128)(2,1)}) %all-gather.25.cloned.1.call-update) | async-done | bytes 2097168 | tf_op jit(solution)/shard_map/all_gather | solution.py:175
  262.9 14.5 fusion.52
  277.4 15.3 %all-gather.43.cloned.1.call-done = bf16[1,1024,1024]{2,1,0:T(8,128)(2,1)} async-done(((bf16[1,1024,128]{2,1,0:T(8,128)(2,1)}), bf16[1,1024,1024]{2,1,0:T(8,128)(2,1)}) %all-gather.43.cloned.1.call-update) | async-done | bytes 2097168 | tf_op jit(solution)/shard_map/all_gather | solution.py:211
  292.7 6.0 convert_bitcast_fusion.4
  299.7 42.5 %reduce-scatter.19.cloned.1.call-done = bf16[256,1,1024]{2,0,1:T(8,128)(2,1)} async-done(((bf16[1024,1,1024]{2,0,1:T(8,128)(2,1)}), bf16[256,1,1024]{2,0,1:T(8,128)(2,1)}) %reduce-scatter.19.cloned.1.call-update) | async-done | bytes 524304 | tf_op jit(solution)/shard_map/reduce_scatter | solution.py:185
  345.0 13.2 all-gather.5
  358.2 12.2 all-gather.45.cloned.1.call-done
  370.4 47.7 %all-gather.27.cloned.1.call-done = bf16[1024,1,1024]{2,0,1:T(8,128)(2,1)} async-done(((bf16[256,1,1024]{2,0,1:T(8,128)(2,1)}), bf16[1024,1,1024]{2,0,1:T(8,128)(2,1)}) %all-gather.27.cloned.1.call-update) | async-done | bytes 2097168 | tf_op jit(solution)/shard_map/all_gather | solution.py:175
  425.5 7.8 concatenate.89
  436.6 26.0 %while.109 = (s32[]{:T(128)}, bf16[4,1024,64]{1,2,0:T(8,128)(2,1)S(1)}, f32[4,1024]{1,0:T(4,128)}, bf16[4,1024,64]{2,1,0:T(8,128)(2,1)S(1)}, bf16[4,1024,64]{2,1...) while((s32[]{:T(128)}, ...), condition=%wide.region_19.20_spmd, body=%wide.region_14.19_spmd.sunk | while | flops 138968576 | bytes 8622382 | solution.py:98
  467.0 41.8 %reduce-scatter.21.cloned.1.call-done = bf16[256,1,1024]{2,0,1:T(8,128)(2,1)} async-done(((bf16[1024,1,1024]{2,0,1:T(8,128)(2,1)}), bf16[256,1,1024]{2,0,1:T(8,128)(2,1)}) %reduce-scatter.21.cloned.1.call-update) | async-done | bytes 524304 | tf_op jit(solution)/shard_map/reduce_scatter | solution.py:185
  514.5 24.7 %all-gather.47.cloned.1.call-done = bf16[1,1024,1024]{2,1,0:T(8,128)(2,1)} async-done(((bf16[1,128,1024]{2,1,0:T(8,128)(2,1)}), bf16[1,1024,1024]{2,1,0:T(8,128)(2,1)}) %all-gather.47.cloned.1.call-update) | async-done | bytes 2097168 | tf_op jit(solution)/shard_map/all_gather | solution.py:210
  539.2 47.6 %all-gather.29.cloned.1.call-done = bf16[1024,1,1024]{2,0,1:T(8,128)(2,1)} async-done(((bf16[256,1,1024]{2,0,1:T(8,128)(2,1)}), bf16[1024,1,1024]{2,0,1:T(8,128)(2,1)}) %all-gather.29.cloned.1.call-update) | async-done | bytes 2097168 | tf_op jit(solution)/shard_map/all_gather | solution.py:175
  586.8 14.5 fusion.55
  601.4 31.7 %all-gather.31.cloned.1.call-done = bf16[1024,1,1024]{2,0,1:T(8,128)(2,1)} async-done(((bf16[256,1,1024]{2,0,1:T(8,128)(2,1)}), bf16[1024,1,1024]{2,0,1:T(8,128)(2,1)}) %all-gather.31.cloned.1.call-update) | async-done | bytes 2097168 | tf_op jit(solution)/shard_map/all_gather | solution.py:178
  633.1 29.3 %all-gather.49.cloned.1.call-done = bf16[1,1024,1024]{2,1,0:T(8,128)(2,1)} async-done(((bf16[1,1024,128]{2,1,0:T(8,128)(2,1)}), bf16[1,1024,1024]{2,1,0:T(8,128)(2,1)}) %all-gather.49.cloned.1.call-update) | async-done | bytes 2097168 | tf_op jit(solution)/shard_map/all_gather | solution.py:211
  662.4 7.2 convert_reduce_fusion
  674.7 5.9 convert_bitcast_fusion.2
  680.7 37.4 %reduce-scatter.25.cloned.1.call-done = bf16[256,1,1024]{2,0,1:T(8,128)(2,1)} async-done(((bf16[1024,1,1024]{2,0,1:T(8,128)(2,1)}), bf16[256,1,1024]{2,0,1:T(8,128)(2,1)}) %reduce-scatter.25.cloned.1.call-update) | async-done | bytes 524304 | tf_op jit(solution)/shard_map/reduce_scatter | solution.py:197
  720.3 43.2 %reduce-scatter.23.cloned.1.call-done = bf16[256,1,1024]{2,0,1:T(8,128)(2,1)} async-done(((bf16[1024,1,1024]{2,0,1:T(8,128)(2,1)}), bf16[256,1,1024]{2,0,1:T(8,128)(2,1)}) %reduce-scatter.23.cloned.1.call-update) | async-done | bytes 524304 | tf_op jit(solution)/shard_map/reduce_scatter | solution.py:185
  763.5 3.9 convert_reduce_fusion.10
  769.5 43.6 %all-gather.33.cloned.1.call-done = bf16[1024,1,1024]{2,0,1:T(8,128)(2,1)} async-done(((bf16[256,1,1024]{2,0,1:T(8,128)(2,1)}), bf16[1024,1,1024]{2,0,1:T(8,128)(2,1)}) %all-gather.33.cloned.1.call-update) | async-done | bytes 2097168 | tf_op jit(solution)/shard_map/all_gather | solution.py:178
  818.0 45.1 %while.111 = (s32[]{:T(128)}, f32[4,1024,64]{1,2,0:T(8,128)}, f32[4,1024,64]{1,2,0:T(8,128)S(1)}, bf16[4,1024,64]{1,2,0:T(8,128)(2,1)S(1)}, bf16[4,1024,64]{2,1,...) while((s32[]{:T(128)}, f32[4,1024,64]{1,2,0:T(8,128)}, ...), condition=%wide.region_31.32_spmd, body=%wide.region_27.31_spmd.sunk | while | flops 340098560 | bytes 21916056 | solution.py:149
  822.7 5.4 while.116
  833.9 5.4 while.116
  845.2 5.4 while.116
  856.5 5.4 while.116
  872.6 4.8 fusion.138
  877.5 42.5 %reduce-scatter.27.cloned.1.call-done = bf16[256,1,1024]{2,0,1:T(8,128)(2,1)} async-done(((bf16[1024,1,1024]{2,0,1:T(8,128)(2,1)}), bf16[256,1,1024]{2,0,1:T(8,128)(2,1)}) %reduce-scatter.27.cloned.1.call-update) | async-done | bytes 524304 | tf_op jit(solution)/shard_map/reduce_scatter | solution.py:197
  925.3 45.3 %all-gather.35.cloned.1.call-done = bf16[1024,1,1024]{2,0,1:T(8,128)(2,1)} async-done(((bf16[256,1,1024]{2,0,1:T(8,128)(2,1)}), bf16[1024,1,1024]{2,0,1:T(8,128)(2,1)}) %all-gather.35.cloned.1.call-update) | async-done | bytes 2097168 | tf_op jit(solution)/shard_map/all_gather | solution.py:178
  970.6 7.2 convert_reduce_fusion.1
  983.1 42.5 %reduce-scatter.29.cloned.1.call-done = bf16[256,1,1024]{2,0,1:T(8,128)(2,1)} async-done(((bf16[1024,1,1024]{2,0,1:T(8,128)(2,1)}), bf16[256,1,1024]{2,0,1:T(8,128)(2,1)}) %reduce-scatter.29.cloned.1.call-update) | async-done | bytes 524304 | tf_op jit(solution)/shard_map/reduce_scatter | solution.py:197
  1031.2 6.6 fusion.93
  1039.6 6.1 fusion.86
  1047.3 6.1 fusion.103
  1055.0 5.9 fusion.117
  1064.5 12.3 all-gather.37.cloned.1.call-done
  1085.1 45.2 %while.113 = (s32[]{:T(128)}, f32[4,1024,64]{1,2,0:T(8,128)}, f32[4,1024,64]{1,2,0:T(8,128)S(1)}, bf16[4,1024,64]{1,2,0:T(8,128)(2,1)S(1)}, bf16[4,1024,64]{2,1,...) while((s32[]{:T(128)}, f32[4,1024,64]{1,2,0:T(8,128)}, ...), condition=%wide.region_42.43_spmd, body=%wide.region_38.42_spmd.sunk | while | flops 340098560 | bytes 21916056 | solution.py:149
  1089.9 5.4 while.117
  1101.2 5.4 while.117
  1112.5 5.4 while.117
  1123.8 5.4 while.117
  1139.3 5.2 fusion.139
  1144.9 5.3 fusion.106
  1151.5 5.1 fusion.120
  1160.8 24.5 %reduce-scatter.45.cloned.1.call-done = f32[1024,128]{1,0:T(8,128)} async-done(((f32[1024,1024]{1,0:T(8,128)}), f32[1024,128]{1,0:T(8,128)}) %reduce-scatter.45.cloned.1.call-update) | async-done | bytes 524304 | tf_op jit(solution)/shard_map/reduce_scatter | solution.py:340
  1187.6 52.6 %reduce-scatter.43.cloned.1.call-done = f32[128,1024]{1,0:T(8,128)} async-done(((f32[1024,1024]{1,0:T(8,128)}), f32[128,1024]{1,0:T(8,128)}) %reduce-scatter.43.cloned.1.call-update) | async-done | bytes 524304 | tf_op jit(solution)/shard_map/reduce_scatter | solution.py:339
  1240.3 54.7 %reduce-scatter.41.cloned.1.call-done = f32[128,1024]{1,0:T(8,128)} async-done(((f32[1024,1024]{1,0:T(8,128)}), f32[128,1024]{1,0:T(8,128)}) %reduce-scatter.41.cloned.1.call-update) | async-done | bytes 524304 | tf_op jit(solution)/shard_map/reduce_scatter | solution.py:339
  1297.5 20.6 %all-reduce.1 = (f32[2,3,256]{2,1,0:T(4,128)S(1)}, f32[2,1024]{1,0:T(2,128)}) all-reduce(f32[2,3,256]{2,1,0:T(4,128)S(1)} %pad_maximum_fusion.13, f32[2,1024]{1,0:T(2,128)S(1)} %pad_maximum_fusion.14), channel_id=1, replica_groups=mesh['dp'=8,'tensor'=4] {'dp'}, use_global_device_ids=true, to_apply=%region_50.51 | all-reduce | flops 3584 | bytes 28672 | tf_op jit(solution)/shard_map/psum | solution.py:350
  1318.7 15.6 %reduce-scatter.39.cloned.1.call-done = f32[256,128]{1,0:T(8,128)} async-done(((f32[256,1024]{1,0:T(8,128)}), f32[256,128]{1,0:T(8,128)}) %reduce-scatter.39.cloned.1.call-update) | async-done | bytes 131088 | tf_op jit(solution)/shard_map/reduce_scatter | solution.py:338
  1334.3 39.4 %reduce-scatter.37.cloned.1.call-done = f32[256,128]{1,0:T(8,128)} async-done(((f32[256,1024]{1,0:T(8,128)}), f32[256,128]{1,0:T(8,128)}) %reduce-scatter.37.cloned.1.call-update) | async-done | bytes 131088 | tf_op jit(solution)/shard_map/reduce_scatter | solution.py:338
  1375.4 44.6 %reduce-scatter.31.cloned.1.call-done = bf16[256,1,1024]{2,0,1:T(8,128)(2,1)} async-done(((bf16[1024,1,1024]{2,0,1:T(8,128)(2,1)}), bf16[256,1,1024]{2,0,1:T(8,128)(2,1)}) %reduce-scatter.31.cloned.1.call-update) | async-done | bytes 524304 | tf_op jit(solution)/shard_map/reduce_scatter | solution.py:197
  1425.2 40.3 %all-reduce = (f32[2,2,1024]{2,1,0:T(2,128)}, f32[2,2,1024]{2,1,0:T(2,128)}, f32[2,2,1024]{2,1,0:T(2,128)}) all-reduce(f32[2,2,1024]{2,1,0:T(2,128)S(1)} %pad_maximum_fusion.10, f32[2,2,1024]{2,1,0:T(2,128)S(1)} %pad_maximum_fusion.11, f32[2,2,1024]{2,1,0:T(2,128)S(1)} %pad_maximum_fusion.12), channel_id=1, replica_groups=mesh['dp'=8,'tensor'=4] {'dp','tensor'}, use_global_device_ids=true, to_apply=%region_64.65 | all-reduce | flops 12288 | bytes 98304 | tf_op jit(solution)/shard_map/psum | solution.py:347
  1465.5 3.9 reduce-scatter.35.cloned.1.call-done
  1469.4 49.8 %reduce-scatter.33.cloned.1.call-done = f32[128,3,256]{2,0,1:T(8,128)} async-done(((f32[1024,3,256]{2,0,1:T(8,128)}), f32[128,3,256]{2,0,1:T(8,128)}) %reduce-scatter.33.cloned.1.call-update) | async-done | bytes 393232 | tf_op jit(solution)/shard_map/reduce_scatter | solution.py:337
  (799 shorter events, 309.3 us)
Async XLA Ops:
  7.2 32.3 %all-gather.39.cloned.1.call-start = ((), (), s32[]{:S(2)}) async-start(), calls=%async_computation.40 | async-start | bytes 1769472 | tf_op jit(solution)/shard_map/all_gather | solution.py:208
  9.9 77.3 %all-gather.23.cloned.1.call-start = ((), (), s32[]{:S(2)}) async-start(), calls=%async_computation.16 | async-start | bytes 2621440 | tf_op jit(solution)/shard_map/all_gather | solution.py:175
  11.1 79.9 %copy-start.71 = (f32[256]{0:T(256)}, f32[256]{0:T(256)S(1)}, u32[]{:S(2)}) copy-start(f32[256]{0:T(256)S(1)} %broadcast_multiply_fusion.11) | copy-start | bytes 3076
  12.5 78.6 %copy-start.88 = (f32[256]{0:T(256)}, f32[256]{0:T(256)S(1)}, u32[]{:S(2)}) copy-start(f32[256]{0:T(256)S(1)} %add_rsqrt_fusion.3) | copy-start | bytes 3076
  14.5 173.1 %copy-start.66 = (f32[1,1,1024]{2,1,0:T(1,128)}, f32[1,1,1024]{2,1,0:T(1,128)S(1)}, u32[]{:S(2)}) copy-start(f32[1,1,1024]{2,1,0:T(1,128)S(1)} %get-tuple-element.803) | copy-start | bytes 12292
  17.3 167.7 %reduce-scatter.17.cloned.1.call-start = ((), (), s32[]{:S(2)}) async-start(), calls=%async_computation.17 | async-start | bytes 2621440 | tf_op jit(solution)/shard_map/reduce_scatter | solution.py:185
  18.0 73.1 %copy-start.104 = (f32[10]{0:T(128)}, f32[10]{0:T(128)S(1)}, u32[]{:S(2)}) copy-start(f32[10]{0:T(128)S(1)} %multiply_power_fusion) | copy-start | bytes 124
  32.3 391.1 %copy-start.16 = (f32[1024,10]{0,1:T(8,128)}, f32[1024,10]{0,1:T(8,128)S(1)}, u32[]{:S(2)}) copy-start(f32[1024,10]{0,1:T(8,128)S(1)} %get-tuple-element.805) | copy-start | bytes 122884
  32.3 391.1 %copy-start.19 = (f32[1024,10]{0,1:T(8,128)}, f32[1024,10]{0,1:T(8,128)S(1)}, u32[]{:S(2)}) copy-start(f32[1024,10]{0,1:T(8,128)S(1)} %get-tuple-element.806) | copy-start | bytes 122884
  32.3 391.1 %copy-start.22 = (f32[1024,10]{0,1:T(8,128)}, f32[1024,10]{0,1:T(8,128)S(1)}, u32[]{:S(2)}) copy-start(f32[1024,10]{0,1:T(8,128)S(1)} %get-tuple-element.807) | copy-start | bytes 122884
  142.4 72.9 %all-gather.41.cloned.1.call-start = ((), (), s32[]{:S(2)}) async-start(), calls=%async_computation.41 | async-start | bytes 2359296 | tf_op jit(solution)/shard_map/all_gather | solution.py:210
  144.3 47.7 %copy-start.87 = (bf16[2,1024]{1,0:T(2,128)(2,1)S(1)}, bf16[2,1024]{1,0:T(2,128)(2,1)}, u32[]{:S(2)}) copy-start(bf16[2,1024]{1,0:T(2,128)(2,1)} %param.37) | copy-start | bytes 12292
  144.3 118.6 %all-gather.25.cloned.1.call-start = ((), (), s32[]{:S(2)}) async-start(), calls=%async_computation.18 | async-start | bytes 2621440 | tf_op jit(solution)/shard_map/all_gather | solution.py:175
  145.0 197.2 %copy-start.57 = (f32[1,1,1024]{2,1,0:T(1,128)}, f32[1,1,1024]{2,1,0:T(1,128)S(1)}, u32[]{:S(2)}) copy-start(f32[1,1,1024]{2,1,0:T(1,128)S(1)} %get-tuple-element.800) | copy-start | bytes 12292
  186.3 91.1 %copy-start.73 = (f32[256]{0:T(256)}, f32[256]{0:T(256)S(1)}, u32[]{:S(2)}) copy-start(f32[256]{0:T(256)S(1)} %broadcast_multiply_fusion.10) | copy-start | bytes 3076
  187.6 89.7 %copy-start.93 = (f32[256]{0:T(256)}, f32[256]{0:T(256)S(1)}, u32[]{:S(2)}) copy-start(f32[256]{0:T(256)S(1)} %add_rsqrt_fusion.2) | copy-start | bytes 3076
  189.8 102.9 %all-gather.43.cloned.1.call-start = ((), (), s32[]{:S(2)}) async-start(), calls=%async_computation.42 | async-start | bytes 2359296 | tf_op jit(solution)/shard_map/all_gather | solution.py:211
  191.8 150.4 %reduce-scatter.19.cloned.1.call-start = ((), (), s32[]{:S(2)}) async-start(), calls=%async_computation.19 | async-start | bytes 2621440 | tf_op jit(solution)/shard_map/reduce_scatter | solution.py:185
  192.6 84.8 %copy-start.100 = (f32[1,1024]{1,0:T(1,128)}, f32[1,1024]{1,0:T(1,128)S(1)}, u32[]{:S(2)}) copy-start(f32[1,1024]{1,0:T(1,128)S(1)} %get-tuple-element.788) | copy-start | bytes 12292
  292.7 49.4 %copy-start.5 = (bf16[256,1,1024]{2,0,1:T(8,128)(2,1)S(1)}, bf16[256,1,1024]{2,0,1:T(8,128)(2,1)}, u32[]{:S(2)}) copy-start(bf16[256,1,1024]{2,0,1:T(8,128)(2,1)} %reduce-scatter.17.cloned.1.call-done) | copy-start | bytes 1572868
  298.7 71.7 %all-gather.45.cloned.1.call-start = ((), (), s32[]{:S(2)}) async-start(), calls=%async_computation.43 | async-start | bytes 1769472 | tf_op jit(solution)/shard_map/all_gather | solution.py:208
  299.6 118.5 %all-gather.27.cloned.1.call-start = ((), (), s32[]{:S(2)}) async-start(), calls=%async_computation.20 | async-start | bytes 2621440 | tf_op jit(solution)/shard_map/all_gather | solution.py:175
  343.6 165.2 %copy-start.3 = (f32[256,1,1024]{2,0,1:T(8,128)}, f32[256,1,1024]{2,0,1:T(8,128)S(1)}, u32[]{:S(2)}) copy-start(f32[256,1,1024]{2,0,1:T(8,128)S(1)} %get-tuple-element.646) | copy-start | bytes 3145732
  343.6 78.4 %copy-start.69 = (f32[256]{0:T(256)}, f32[256]{0:T(256)S(1)}, u32[]{:S(2)}) copy-start(f32[256]{0:T(256)S(1)} %broadcast_multiply_fusion.9) | copy-start | bytes 3076
  343.8 78.2 %copy-start.75 = (f32[256]{0:T(256)}, f32[256]{0:T(256)S(1)}, u32[]{:S(2)}) copy-start(f32[256]{0:T(256)S(1)} %add_rsqrt_fusion.1) | copy-start | bytes 3076
  344.9 163.8 %reduce-scatter.21.cloned.1.call-start = ((), (), s32[]{:S(2)}) async-start(), calls=%async_computation.21 | async-start | bytes 2621440 | tf_op jit(solution)/shard_map/reduce_scatter | solution.py:185
  462.6 47.4 %copy-start.30 = (bf16[4,1024,64]{1,2,0:T(8,128)(2,1)}, bf16[4,1024,64]{1,2,0:T(8,128)(2,1)S(1)}, u32[]{:S(2)}) copy-start(bf16[4,1024,64]{1,2,0:T(8,128)(2,1)S(1)} %get-tuple-element.340) | copy-start | bytes 1572868
  466.2 73.0 %all-gather.47.cloned.1.call-start = ((), (), s32[]{:S(2)}) async-start(), calls=%async_computation.44 | async-start | bytes 2359296 | tf_op jit(solution)/shard_map/all_gather | solution.py:210
  466.9 119.9 %all-gather.29.cloned.1.call-start = ((), (), s32[]{:S(2)}) async-start(), calls=%async_computation.22 | async-start | bytes 2621440 | tf_op jit(solution)/shard_map/all_gather | solution.py:175
  510.0 76.8 %copy-start.103 = (f32[1,1024]{1,0:T(1,128)S(1)}, f32[1,1024]{1,0:T(1,128)}, u32[]{:S(2)}) copy-start(f32[1,1024]{1,0:T(1,128)} %get-tuple-element.787) | copy-start | bytes 12292
  511.4 121.7 %all-gather.31.cloned.1.call-start = ((), (), s32[]{:S(2)}) async-start(), calls=%async_computation.24 | async-start | bytes 2621440 | tf_op jit(solution)/shard_map/all_gather | solution.py:178
  513.6 148.8 %all-gather.49.cloned.1.call-start = ((), (), s32[]{:S(2)}) async-start(), calls=%async_computation.45 | async-start | bytes 2359296 | tf_op jit(solution)/shard_map/all_gather | solution.py:211
  514.2 203.9 %reduce-scatter.25.cloned.1.call-start = ((), (), s32[]{:S(2)}) async-start(), calls=%async_computation.25 | async-start | bytes 2621440 | tf_op jit(solution)/shard_map/reduce_scatter | solution.py:197
  674.7 88.8 %reduce-scatter.23.cloned.1.call-start = ((), (), s32[]{:S(2)}) async-start(), calls=%async_computation.23 | async-start | bytes 2621440 | tf_op jit(solution)/shard_map/reduce_scatter | solution.py:185
  680.6 82.9 %copy-start.92 = (f32[1,1,1024]{2,1,0:T(1,128)S(1)}, f32[1,1,1024]{2,1,0:T(1,128)}, u32[]{:S(2)}) copy-start(f32[1,1,1024]{2,1,0:T(1,128)} %get-tuple-element.769) | copy-start | bytes 12292
  680.6 132.4 %all-gather.33.cloned.1.call-start = ((), (), s32[]{:S(2)}) async-start(), calls=%async_computation.26 | async-start | bytes 2621440 | tf_op jit(solution)/shard_map/all_gather | solution.py:178
  763.5 49.6 %copy-start.37 = (bf16[1,256,1024]{2,1,0:T(8,128)(2,1)S(1)}, bf16[1,256,1024]{2,1,0:T(8,128)(2,1)}, u32[]{:S(2)}) copy-start(bf16[1,256,1024]{2,1,0:T(8,128)(2,1)} %all-gather.5) | copy-start | bytes 1572868
  767.5 152.5 %reduce-scatter.27.cloned.1.call-start = ((), (), s32[]{:S(2)}) async-start(), calls=%async_computation.27 | async-start | bytes 2621440 | tf_op jit(solution)/shard_map/reduce_scatter | solution.py:197
  768.0 47.4 %copy-start.10 = (bf16[4,1024,64]{1,2,0:T(8,128)(2,1)}, bf16[4,1024,64]{1,2,0:T(8,128)(2,1)S(1)}, u32[]{:S(2)}) copy-start(bf16[4,1024,64]{1,2,0:T(8,128)(2,1)S(1)} %fusion.207) | copy-start | bytes 1572868
  872.6 47.4 %copy-start.4 = (f32[256,1,1024]{2,0,1:T(8,128)S(1)}, f32[256,1,1024]{2,0,1:T(8,128)}, u32[]{:S(2)}) copy-start(f32[256,1,1024]{2,0,1:T(8,128)} %copy-done.3) | copy-start | bytes 3145732
  872.6 47.4 %copy-start.65 = (f32[1,1,1024]{2,1,0:T(1,128)S(1)}, f32[1,1,1024]{2,1,0:T(1,128)}, u32[]{:S(2)}) copy-start(f32[1,1,1024]{2,1,0:T(1,128)} %get-tuple-element.772) | copy-start | bytes 12292
  872.6 47.4 %copy-start.70 = (f32[256]{0:T(256)S(1)}, f32[256]{0:T(256)}, u32[]{:S(2)}) copy-start(f32[256]{0:T(256)} %copy-done.69) | copy-start | bytes 3076
  872.6 47.4 %copy-start.76 = (f32[256]{0:T(256)S(1)}, f32[256]{0:T(256)}, u32[]{:S(2)}) copy-start(f32[256]{0:T(256)} %copy-done.75) | copy-start | bytes 3076
  877.4 93.2 %copy-start.101 = (f32[1,1024]{1,0:T(1,128)S(1)}, f32[1,1024]{1,0:T(1,128)}, u32[]{:S(2)}) copy-start(f32[1,1024]{1,0:T(1,128)} %copy-done.100) | copy-start | bytes 12292
  877.4 93.2 %all-gather.35.cloned.1.call-start = ((), (), s32[]{:S(2)}) async-start(), calls=%async_computation.28 | async-start | bytes 2621440 | tf_op jit(solution)/shard_map/all_gather | solution.py:178
  925.1 100.5 %reduce-scatter.29.cloned.1.call-start = ((), (), s32[]{:S(2)}) async-start(), calls=%async_computation.29 | async-start | bytes 2621440 | tf_op jit(solution)/shard_map/reduce_scatter | solution.py:197
  983.0 93.8 %all-gather.37.cloned.1.call-start = ((), (), s32[]{:S(2)}) async-start(), calls=%async_computation.30 | async-start | bytes 2621440 | tf_op jit(solution)/shard_map/all_gather | solution.py:178
  1031.2 129.6 %reduce-scatter.47.cloned.1.call-start = ((), (), s32[]{:S(2)}) async-start(), calls=%async_computation.39 | async-start | bytes 4718592 | tf_op jit(solution)/shard_map/reduce_scatter | solution.py:340
  1037.9 147.4 %reduce-scatter.45.cloned.1.call-start = ((), (), s32[]{:S(2)}) async-start(), calls=%async_computation.38 | async-start | bytes 4718592 | tf_op jit(solution)/shard_map/reduce_scatter | solution.py:340
  1045.7 194.6 %reduce-scatter.43.cloned.1.call-start = ((), (), s32[]{:S(2)}) async-start(), calls=%async_computation.37 | async-start | bytes 4718592 | tf_op jit(solution)/shard_map/reduce_scatter | solution.py:339
  1053.4 241.5 %reduce-scatter.41.cloned.1.call-start = ((), (), s32[]{:S(2)}) async-start(), calls=%async_computation.36 | async-start | bytes 4718592 | tf_op jit(solution)/shard_map/reduce_scatter | solution.py:339
  1060.9 273.3 %reduce-scatter.39.cloned.1.call-start = ((), (), s32[]{:S(2)}) async-start(), calls=%async_computation.35 | async-start | bytes 1179648 | tf_op jit(solution)/shard_map/reduce_scatter | solution.py:338
  1064.4 309.3 %reduce-scatter.37.cloned.1.call-start = ((), (), s32[]{:S(2)}) async-start(), calls=%async_computation.34 | async-start | bytes 1179648 | tf_op jit(solution)/shard_map/reduce_scatter | solution.py:338
  1083.9 336.1 %reduce-scatter.31.cloned.1.call-start = ((), (), s32[]{:S(2)}) async-start(), calls=%async_computation.31 | async-start | bytes 2621440 | tf_op jit(solution)/shard_map/reduce_scatter | solution.py:197
  1144.5 324.8 %reduce-scatter.35.cloned.1.call-start = ((), (), s32[]{:S(2)}) async-start(), calls=%async_computation.33 | async-start | bytes 3538944 | tf_op jit(solution)/shard_map/reduce_scatter | solution.py:337
  1150.1 369.0 %reduce-scatter.33.cloned.1.call-start = ((), (), s32[]{:S(2)}) async-start(), calls=%async_computation.32 | async-start | bytes 3538944 | tf_op jit(solution)/shard_map/reduce_scatter | solution.py:337
  1160.3 137.0 %copy-start.29 = (bf16[1024,1,4,64]{0,3,2,1:T(8,128)(2,1)S(1)}, bf16[1024,1,4,64]{0,3,2,1:T(8,128)(2,1)}, u32[]{:S(2)}) copy-start(bf16[1024,1,4,64]{0,3,2,1:T(8,128)(2,1)} %copy-done.28) | copy-start | bytes 1572868
  1185.3 234.6 %copy-start.2 = (bf16[256,1,1024]{2,0,1:T(8,128)(2,1)S(1)}, bf16[256,1,1024]{2,0,1:T(8,128)(2,1)}, u32[]{:S(2)}) copy-start(bf16[256,1,1024]{2,0,1:T(8,128)(2,1)} %param.29) | copy-start | bytes 1572868
  1185.3 234.6 %copy-start.63 = (f32[1,1,1024]{2,1,0:T(1,128)S(1)}, f32[1,1,1024]{2,1,0:T(1,128)}, u32[]{:S(2)}) copy-start(f32[1,1,1024]{2,1,0:T(1,128)} %copy-done.62) | copy-start | bytes 12292
  1185.3 234.6 %copy-start.72 = (f32[256]{0:T(256)S(1)}, f32[256]{0:T(256)}, u32[]{:S(2)}) copy-start(f32[256]{0:T(256)} %copy-done.71) | copy-start | bytes 3076
  1185.3 234.6 %copy-start.89 = (f32[256]{0:T(256)S(1)}, f32[256]{0:T(256)}, u32[]{:S(2)}) copy-start(f32[256]{0:T(256)} %copy-done.88) | copy-start | bytes 3076
  1187.6 233.9 %copy-start.33 = (f32[256,1,1024]{2,0,1:T(8,128)S(1)}, f32[256,1,1024]{2,0,1:T(8,128)}, u32[]{:S(2)}) copy-start(f32[256,1,1024]{2,0,1:T(8,128)} %get-tuple-element.634) | copy-start | bytes 3145732
  1375.4 49.7 %copy-start.81 = (f32[1024]{0:T(1024)S(1)}, f32[1024]{0:T(1024)}, u32[]{:S(2)}) copy-start(f32[1024]{0:T(1024)} %get-tuple-element.491) | copy-start | bytes 12292
  1375.4 49.7 %copy-start.80 = (f32[1024]{0:T(1024)S(1)}, f32[1024]{0:T(1024)}, u32[]{:S(2)}) copy-start(f32[1024]{0:T(1024)} %get-tuple-element.504) | copy-start | bytes 12292
  (79 other events, 1202.8 us)
Sparse Core Ops, SparseCore 0:
  10.5 28.9 all-gather.38
  41.7 45.5 all-gather.22
  142.5 42.4 reduce-scatter.16
  187.4 27.7 all-gather.40
  217.3 45.4 all-gather.24
  265.3 27.3 all-gather.42
  298.8 43.2 reduce-scatter.18
  344.6 25.7 all-gather.44
  372.6 45.5 all-gather.26
  466.3 42.4 reduce-scatter.20
  511.4 27.7 all-gather.46
  541.3 45.4 all-gather.28
  588.5 44.5 all-gather.30
  635.0 27.3 all-gather.48
  674.8 43.2 reduce-scatter.24
  720.3 43.1 reduce-scatter.22
  767.6 45.4 all-gather.32
  877.5 42.4 reduce-scatter.26
  925.2 45.3 all-gather.34
  983.1 42.3 reduce-scatter.28
  1031.3 45.4 all-gather.36
  1080.5 50.0 reduce-scatter.46
  1134.0 51.2 reduce-scatter.44
  1188.9 51.3 reduce-scatter.42
  1243.6 51.2 reduce-scatter.40
  1298.3 35.9 reduce-scatter.38
  1337.6 36.0 reduce-scatter.36
  1376.1 43.8 reduce-scatter.30
  1423.3 45.9 reduce-scatter.34
  1473.0 46.1 reduce-scatter.32
where the time goes:
time: 1540 us; the launch traced here: 1530 us
  waiting for transfers between devices  1010 us (66%)
  matrix products  190 us (12%)
  local copies, waits for them, and re-layouts  148 us (10%)
  blocking collectives  87 us (6%)
  other arithmetic  69.1 us (4%)
  between operations  17.1 us (1%)
    all_gather x4, waiting for transfers between devices, spread_rows(): return lax.all_gather(normed, 'tensor', axis=0, tiled=True)  191 us
    reduce_scatter x4, waiting for transfers between devices, collect_rows(): lax.psum_scatter(partial_term(jnp.int32(0), row_count * lax.axis_size('te...  167 us
    reduce_scatter x4, waiting for transfers between devices, collect_grads(): lax.psum_scatter(partial_term(jnp.int32(0), row_count * lax.axis_size('te...  167 us
    all_gather x4, waiting for transfers between devices, spread_grads(): return lax.all_gather(upstream_low, 'tensor', axis=0, tiled=True)  133 us
    reduce_scatter x2, waiting for transfers between devices, shards(): lax.psum_scatter(expand_grad, 'dp', scatter_dimension=0, tiled=True)  107 us
    reduce_scatter x2, waiting for transfers between devices, shards(): lax.psum_scatter(exit_grad, 'dp', scatter_dimension=1, tiled=True)  55 us
    reduce_scatter x2, waiting for transfers between devices, shards(): lax.psum_scatter(triple_grad, 'dp', scatter_dimension=0, tiled=True)  53.7 us
    all_gather x2, waiting for transfers between devices, shards(): lax.all_gather(expand_weight[layer_index], 'dp', axis=0, tiled=True)  47.3 us
  transfers between devices with their start and end apart: 30, of which 29 were waited for; matrix products, arithmetic and copies ran while one was open for 12% of the time, Pallas kernels for 0%

commit v1 on v0

--- a/solution.py
+++ b/solution.py
@@ -8,6 +8,15 @@
 LAYERS = 2
 SEQ = 1024
 QBLOCK = 512
+
+
+DP = ("dh", "th")
+TP = ("b", "tl")
+SWAP = [(0, 0), (1, 2), (2, 1), (3, 3)]
+
+
+def swap(array):
+    return lax.ppermute(array, ("b", "th"), SWAP)
 
 
 EPSILON = 1e-06
@@ -164,6 +173,20 @@
     norm_shift,
     branch_bias,
 ):
+    tokens, cotangent, clip_mask, positions = [
+        swap(array) for array in (tokens, cotangent, clip_mask, positions)
+    ]
+    triple_weight, triple_bias, exit_weight, expand_weight, expand_bias, shrink_weight = [
+        swap(array)
+        for array in (
+            triple_weight,
+            triple_bias,
+            exit_weight,
+            expand_weight,
+            expand_bias,
+            shrink_weight,
+        )
+    ]
     row_count = tokens.shape[0]
     clip_count = tokens.shape[1]
     local_width = triple_weight.shape[3]
@@ -172,10 +195,10 @@
     live = clip_mask.astype(jnp.float32)[None, :, None]
 
     def spread_rows(normed):
-        return lax.all_gather(normed, "tensor", axis=0, tiled=True)
+        return lax.all_gather(normed, TP, axis=0, tiled=True)
 
     def spread_grads(upstream_low):
-        return lax.all_gather(upstream_low, "tensor", axis=0, tiled=True)
+        return lax.all_gather(upstream_low, TP, axis=0, tiled=True)
 
     def collect_rows(operand, matrix, pattern):
 
@@ -183,8 +206,8 @@
             return jnp.einsum(pattern, operand, matrix, preferred_element_type=jnp.float32)
 
         return lax.psum_scatter(
-            partial_term(jnp.int32(0), row_count * lax.axis_size("tensor")).astype(jnp.bfloat16),
-            "tensor",
+            partial_term(jnp.int32(0), row_count * lax.axis_size(TP)).astype(jnp.bfloat16),
+            TP,
             scatter_dimension=0,
             tiled=True,
         ).astype(jnp.float32)
@@ -195,8 +218,8 @@
             return jnp.einsum(pattern, operand, matrix, preferred_element_type=jnp.float32)
 
         return lax.psum_scatter(
-            partial_term(jnp.int32(0), row_count * lax.axis_size("tensor")).astype(jnp.bfloat16),
-            "tensor",
+            partial_term(jnp.int32(0), row_count * lax.axis_size(TP)).astype(jnp.bfloat16),
+            TP,
             scatter_dimension=0,
             tiled=True,
         ).astype(jnp.float32)
@@ -205,10 +228,10 @@
     saved = []
     for layer_index in range(LAYERS):
         fetched = (
-            lax.all_gather(triple_weight[layer_index], "dp", axis=0, tiled=True),
-            lax.all_gather(exit_weight[layer_index], "dp", axis=1, tiled=True),
-            lax.all_gather(expand_weight[layer_index], "dp", axis=0, tiled=True),
-            lax.all_gather(shrink_weight[layer_index], "dp", axis=1, tiled=True),
+            lax.all_gather(triple_weight[layer_index], DP, axis=0, tiled=True),
+            lax.all_gather(exit_weight[layer_index], DP, axis=1, tiled=True),
+            lax.all_gather(expand_weight[layer_index], DP, axis=0, tiled=True),
+            lax.all_gather(shrink_weight[layer_index], DP, axis=1, tiled=True),
         )
         triple_full, exit_full, expand_full, shrink_full = fetched
         gain_pair = norm_gain[layer_index].astype(jnp.float32)
@@ -277,10 +300,10 @@
             fetched,
         ) = saved[layer_index]
         triple_full, exit_full, expand_full, shrink_full = (
-            lax.all_gather(triple_weight[layer_index], "dp", axis=0, tiled=True),
-            lax.all_gather(exit_weight[layer_index], "dp", axis=1, tiled=True),
-            lax.all_gather(expand_weight[layer_index], "dp", axis=0, tiled=True),
-            lax.all_gather(shrink_weight[layer_index], "dp", axis=1, tiled=True),
+            lax.all_gather(triple_weight[layer_index], DP, axis=0, tiled=True),
+            lax.all_gather(exit_weight[layer_index], DP, axis=1, tiled=True),
+            lax.all_gather(expand_weight[layer_index], DP, axis=0, tiled=True),
+            lax.all_gather(shrink_weight[layer_index], DP, axis=1, tiled=True),
         )
         gain_pair = norm_gain[layer_index].astype(jnp.float32)
         shrink_low = upstream.astype(jnp.bfloat16)
@@ -334,10 +357,10 @@
         shift_parts[layer_index] = jnp.stack([shift_one, shift_two])
         bias_parts[layer_index] = jnp.stack([bias_one, bias_two])
         collected[layer_index] = (
-            lax.psum_scatter(triple_grad, "dp", scatter_dimension=0, tiled=True),
-            lax.psum_scatter(exit_grad, "dp", scatter_dimension=1, tiled=True),
-            lax.psum_scatter(expand_grad, "dp", scatter_dimension=0, tiled=True),
-            lax.psum_scatter(shrink_grad, "dp", scatter_dimension=1, tiled=True),
+            lax.psum_scatter(triple_grad.astype(jnp.bfloat16), DP, scatter_dimension=0, tiled=True).astype(jnp.float32),
+            lax.psum_scatter(exit_grad.astype(jnp.bfloat16), DP, scatter_dimension=1, tiled=True).astype(jnp.float32),
+            lax.psum_scatter(expand_grad.astype(jnp.bfloat16), DP, scatter_dimension=0, tiled=True).astype(jnp.float32),
+            lax.psum_scatter(shrink_grad.astype(jnp.bfloat16), DP, scatter_dimension=1, tiled=True).astype(jnp.float32),
         )
     stacked = [
         jnp.stack([collected[layer_index][member] for layer_index in range(LAYERS)])
@@ -345,20 +368,20 @@
     ]
     triple_total, exit_total, expand_total, shrink_total = stacked
     gain_total, shift_total, bias_total = lax.psum(
-        (jnp.stack(gain_parts), jnp.stack(shift_parts), jnp.stack(bias_parts)), ("dp", "tensor")
+        (jnp.stack(gain_parts), jnp.stack(shift_parts), jnp.stack(bias_parts)), DP + TP
     )
     triple_bias_total, expand_bias_total = lax.psum(
-        (jnp.stack(triple_bias_parts), jnp.stack(expand_bias_parts)), "dp"
+        (jnp.stack(triple_bias_parts), jnp.stack(expand_bias_parts)), DP
     )
     return (
-        mixed,
-        upstream,
-        triple_total,
-        triple_bias_total,
-        exit_total,
-        expand_total,
-        expand_bias_total,
-        shrink_total,
+        swap(mixed),
+        swap(upstream),
+        swap(triple_total),
+        swap(triple_bias_total),
+        swap(exit_total),
+        swap(expand_total),
+        swap(expand_bias_total),
+        swap(shrink_total),
         gain_total,
         shift_total,
         bias_total,
@@ -366,33 +389,36 @@
 
 
 def solution(mesh):
+    shape = (mesh.shape["dp"] // 2, 2, mesh.shape["tensor"] // 2, 2)
+    fine = jax.sharding.Mesh(mesh.devices.reshape(shape), ("dh", "b", "th", "tl"))
+    dp, tensor = ("dh", "b"), ("th", "tl")
     return jax.shard_map(
         shards,
-        mesh=mesh,
+        mesh=fine,
         in_specs=(
-            P("tensor", "dp", None),
-            P("tensor", "dp", None),
-            P("dp"),
-            P(None, "dp", None),
-            P(None, "dp", None, "tensor"),
-            P(None, None, "tensor"),
-            P(None, "tensor", "dp"),
-            P(None, "dp", "tensor"),
-            P(None, "tensor"),
-            P(None, "tensor", "dp"),
+            P(tensor, dp, None),
+            P(tensor, dp, None),
+            P(dp),
+            P(None, dp, None),
+            P(None, dp, None, tensor),
+            P(None, None, tensor),
+            P(None, tensor, dp),
+            P(None, dp, tensor),
+            P(None, tensor),
+            P(None, tensor, dp),
             P(),
             P(),
             P(),
         ),
         out_specs=(
-            P("tensor", "dp", None),
-            P("tensor", "dp", None),
-            P(None, "dp", None, "tensor"),
-            P(None, None, "tensor"),
-            P(None, "tensor", "dp"),
-            P(None, "dp", "tensor"),
-            P(None, "tensor"),
-            P(None, "tensor", "dp"),
+            P(tensor, dp, None),
+            P(tensor, dp, None),
+            P(None, dp, None, tensor),
+            P(None, None, tensor),
+            P(None, tensor, dp),
+            P(None, dp, tensor),
+            P(None, tensor),
+            P(None, tensor, dp),
             P(),
             P(),
             P(),

time: 1540 us -> 2190 us (1.42)
  waiting for transfers between devices: 1010 us -> 1400 us
  matrix products: 190 us -> 282 us
  starting transfers between devices: 2.77 us -> 65.9 us
  local copies, waits for them, and re-layouts: 148 us -> 203 us
  blocking collectives: 87 us -> 140 us
    ppermute x0 -> x18, waiting for transfers between devices: none -> 152 us  [swap(): return lax.ppermute(array, ('b', 'th'), SWAP)]
    reduce_scatter x16 -> x12, waiting for transfers between devices: 575 us -> 670 us  [the longest x2 196 us: shards(): lax.psum_scatter(expand_grad.astype(jnp.bfloat16), DP, scatter_dimension=...]
    unnamed x30 -> x34, waiting for transfers between devices: 1.66 us -> 75.1 us
    all_gather x14, waiting for transfers between devices: 435 us -> 502 us  [the longest x4 180 us: spread_rows(): return lax.all_gather(normed, TP, axis=0, tiled=True)]
    ppermute x0 -> x18, starting transfers between devices: none -> 63.7 us  [swap(): return lax.ppermute(array, ('b', 'th'), SWAP)]
    all_gather x2, blocking collectives: 26.1 us -> 75.2 us  [shards(): lax.all_gather(exit_weight[layer_index], DP, axis=1, tiled=True)]
    dot_general x16, matrix products: 6.05 us -> 32.2 us  [one_block(): jnp.einsum('qk,qe->ke', score_grad, query_block, preferred_element_type=j...]
    dot_general x16, matrix products: 6.02 us -> 32.2 us  [one_block(): jnp.einsum('qk,qe->ke', chances.astype(jnp.bfloat16), grad_block, preferr...]
  transfers between devices with their start and end apart: 30 -> 48, of which waited for: 29 -> 37; matrix products, arithmetic and copies ran while one was open for 12% -> 12% of each run, Pallas kernels for 0% -> 0%
where the time goes in v1:
time: 2190 us; the launch traced here: 2170 us
  waiting for transfers between devices  1400 us (64%)
  matrix products  282 us (13%)
  local copies, waits for them, and re-layouts  203 us (9%)
  blocking collectives  140 us (6%)
  starting transfers between devices  65.9 us (3%)
  other arithmetic  63.8 us (3%)
    reduce_scatter x2, waiting for transfers between devices, shards(): lax.psum_scatter(expand_grad.astype(jnp.bfloat16), DP, scatter_dimension=...  196 us
    all_gather x4, waiting for transfers between devices, spread_rows(): return lax.all_gather(normed, TP, axis=0, tiled=True)  180 us
    reduce_scatter x4, waiting for transfers between devices, collect_grads(): lax.psum_scatter(partial_term(jnp.int32(0), row_count * lax.axis_size(TP)...  170 us
    reduce_scatter x4, waiting for transfers between devices, collect_rows(): lax.psum_scatter(partial_term(jnp.int32(0), row_count * lax.axis_size(TP)...  153 us
    ppermute x18, waiting for transfers between devices, swap(): return lax.ppermute(array, ('b', 'th'), SWAP)  152 us
    reduce_scatter x2, waiting for transfers between devices, shards(): lax.psum_scatter(triple_grad.astype(jnp.bfloat16), DP, scatter_dimension=...  151 us
    all_gather x4, waiting for transfers between devices, spread_grads(): return lax.all_gather(upstream_low, TP, axis=0, tiled=True)  124 us
    all_gather x2, waiting for transfers between devices, shards(): lax.all_gather(shrink_weight[layer_index], DP, axis=1, tiled=True)  118 us
  transfers between devices with their start and end apart: 48, of which 37 were waited for; matrix products, arithmetic and copies ran while one was open for 12% of the time, Pallas kernels for 0%

profile of v1, /device:TPU:1, one launch (start us, length us, event | category | flops | bytes accessed | tf_op | source)
XLA Modules:
  0.0 2172.3 jit_solution(4912255333204654900)
XLA Ops:
  8.5 5.6 collective-permute-start.1
  14.1 9.7 collective-permute-done.1
  29.2 12.7 collective-permute-done
  59.2 38.0 %all-gather.1 = bf16[1,256,1024]{2,1,0:T(8,128)(2,1)} all-gather(bf16[1,256,128]{2,1,0:T(8,128)(2,1)S(1)} %get-tuple-element.807), channel_id=3, replica_groups=mesh['dh'=4,'b'=2,'th'=2,'tl'=2] {'dh','th'}, dimensions={2}, use_global_device_ids=true | all-gather | bytes 589824 | tf_op jit(solution)/shard_map/all_gather | solution.py:232
  97.2 45.7 %all-gather.23.cloned.1.call-done = bf16[1024,1,1024]{2,0,1:T(8,128)(2,1)} async-done(((bf16[256,1,1024]{2,0,1:T(8,128)(2,1)}), bf16[1024,1,1024]{2,0,1:T(8,128)(2,1)}) %all-gather.23.cloned.1.call-update) | async-done | bytes 2097168 | tf_op jit(solution)/shard_map/all_gather | solution.py:198
  155.8 40.4 %while.107 = (s32[]{:T(128)}, bf16[4,1024,64]{1,2,0:T(8,128)(2,1)}, f32[4,1024]{1,0:T(4,128)}, bf16[4,1024,64]{2,1,0:T(8,128)(2,1)}, bf16[4,1024,64]{2,1,0:T(8,1...) while((s32[]{:T(128)}, bf16[4,1024,64]{1,2,0:T(8,128)(2,1)}, ...), condition=%wide.region_7.8_spmd, body=%wide.region_2.7_spmd.sunk | while | flops 138968576 | bytes 8492310 | solution.py:107
  157.8 4.8 while.114
  167.9 4.8 while.114
  178.0 4.8 while.114
  204.4 15.5 collective-permute-done.5
  221.4 26.7 %reduce-scatter.25.cloned.1.call-done = bf16[256,1,1024]{2,0,1:T(8,128)(2,1)} async-done(((bf16[1024,1,1024]{2,0,1:T(8,128)(2,1)}), bf16[256,1,1024]{2,0,1:T(8,128)(2,1)}) %reduce-scatter.25.cloned.1.call-update) | async-done | bytes 524304 | tf_op jit(solution)/shard_map/reduce_scatter | solution.py:208
  254.9 18.0 collective-permute-done.7
  275.9 5.3 collective-permute-done.6
  281.9 24.8 %all-gather.41.cloned.1.call-done = bf16[1,1024,1024]{2,1,0:T(8,128)(2,1)} async-done(((bf16[1,128,1024]{2,1,0:T(8,128)(2,1)}), bf16[1,1024,1024]{2,1,0:T(8,128)(2,1)}) %all-gather.41.cloned.1.call-update) | async-done | bytes 2097168 | tf_op jit(solution)/shard_map/all_gather | solution.py:233
  306.6 45.0 %all-gather.25.cloned.1.call-done = bf16[1024,1,1024]{2,0,1:T(8,128)(2,1)} async-done(((bf16[256,1,1024]{2,0,1:T(8,128)(2,1)}), bf16[1024,1,1024]{2,0,1:T(8,128)(2,1)}) %all-gather.25.cloned.1.call-update) | async-done | bytes 2097168 | tf_op jit(solution)/shard_map/all_gather | solution.py:198
  351.6 14.2 fusion.52
  365.8 51.7 %all-gather.43.cloned.1.call-done = bf16[1,1024,1024]{2,1,0:T(8,128)(2,1)} async-done(((bf16[1,1024,128]{2,1,0:T(8,128)(2,1)}), bf16[1,1024,1024]{2,1,0:T(8,128)(2,1)}) %all-gather.43.cloned.1.call-update) | async-done | bytes 2097168 | tf_op jit(solution)/shard_map/all_gather | solution.py:234
  417.6 5.3 convert_bitcast_fusion.4
  423.7 41.2 %reduce-scatter.27.cloned.1.call-done = bf16[256,1,1024]{2,0,1:T(8,128)(2,1)} async-done(((bf16[1024,1,1024]{2,0,1:T(8,128)(2,1)}), bf16[256,1,1024]{2,0,1:T(8,128)(2,1)}) %reduce-scatter.27.cloned.1.call-update) | async-done | bytes 524304 | tf_op jit(solution)/shard_map/reduce_scatter | solution.py:208
  468.4 37.3 %all-gather.5 = bf16[1,256,1024]{2,1,0:T(8,128)(2,1)} all-gather(bf16[1,256,128]{2,1,0:T(8,128)(2,1)S(1)} %copy-done.47), channel_id=7, replica_groups=mesh['dh'=4,'b'=2,'th'=2,'tl'=2] {'dh','th'}, dimensions={2}, use_global_device_ids=true | all-gather | bytes 589824 | tf_op jit(solution)/shard_map/all_gather | solution.py:232
  505.7 23.1 %all-gather.45.cloned.1.call-done = bf16[1,1024,3,256]{1,3,2,0:T(8,128)(2,1)} async-done(((bf16[1,128,3,256]{1,3,2,0:T(8,128)(2,1)}), bf16[1,1024,3,256]{1,3,2,0:T(8,128)(2,1)}) %all-gather.45.cloned.1.call-update) | async-done | bytes 1572880 | tf_op jit(solution)/shard_map/all_gather | solution.py:231
  528.8 44.5 %all-gather.27.cloned.1.call-done = bf16[1024,1,1024]{2,0,1:T(8,128)(2,1)} async-done(((bf16[256,1,1024]{2,0,1:T(8,128)(2,1)}), bf16[1024,1,1024]{2,0,1:T(8,128)(2,1)}) %all-gather.27.cloned.1.call-update) | async-done | bytes 2097168 | tf_op jit(solution)/shard_map/all_gather | solution.py:198
  586.9 31.9 %while.109 = (s32[]{:T(128)}, bf16[4,1024,64]{1,2,0:T(8,128)(2,1)}, f32[4,1024]{1,0:T(4,128)}, bf16[4,1024,64]{2,1,0:T(8,128)(2,1)}, bf16[4,1024,64]{2,1,0:T(8,1...) while((s32[]{:T(128)}, bf16[4,1024,64]{1,2,0:T(8,128)(2,1)}, ...), condition=%wide.region_19.20_spmd, body=%wide.region_14.19_spmd.sunk | while | flops 138968576 | bytes 8622874 | solution.py:107
  622.8 42.2 %reduce-scatter.29.cloned.1.call-done = bf16[256,1,1024]{2,0,1:T(8,128)(2,1)} async-done(((bf16[1024,1,1024]{2,0,1:T(8,128)(2,1)}), bf16[256,1,1024]{2,0,1:T(8,128)(2,1)}) %reduce-scatter.29.cloned.1.call-update) | async-done | bytes 524304 | tf_op jit(solution)/shard_map/reduce_scatter | solution.py:208
  674.2 14.2 collective-permute-done.8
  691.4 32.6 %all-gather.47.cloned.1.call-done = bf16[1,1024,1024]{2,1,0:T(8,128)(2,1)} async-done(((bf16[1,128,1024]{2,1,0:T(8,128)(2,1)}), bf16[1,1024,1024]{2,1,0:T(8,128)(2,1)}) %all-gather.47.cloned.1.call-update) | async-done | bytes 2097168 | tf_op jit(solution)/shard_map/all_gather | solution.py:233
  724.0 44.4 %all-gather.29.cloned.1.call-done = bf16[1024,1,1024]{2,0,1:T(8,128)(2,1)} async-done(((bf16[256,1,1024]{2,0,1:T(8,128)(2,1)}), bf16[1024,1,1024]{2,0,1:T(8,128)(2,1)}) %all-gather.29.cloned.1.call-update) | async-done | bytes 2097168 | tf_op jit(solution)/shard_map/all_gather | solution.py:198
  768.4 14.5 fusion.55
  782.9 31.1 %all-gather.31.cloned.1.call-done = bf16[1024,1,1024]{2,0,1:T(8,128)(2,1)} async-done(((bf16[256,1,1024]{2,0,1:T(8,128)(2,1)}), bf16[1024,1,1024]{2,0,1:T(8,128)(2,1)}) %all-gather.31.cloned.1.call-update) | async-done | bytes 2097168 | tf_op jit(solution)/shard_map/all_gather | solution.py:201
  813.9 65.9 %all-gather.49.cloned.1.call-done = bf16[1,1024,1024]{2,1,0:T(8,128)(2,1)} async-done(((bf16[1,1024,128]{2,1,0:T(8,128)(2,1)}), bf16[1,1024,1024]{2,1,0:T(8,128)(2,1)}) %all-gather.49.cloned.1.call-update) | async-done | bytes 2097168 | tf_op jit(solution)/shard_map/all_gather | solution.py:234
  879.9 7.2 convert_reduce_fusion
  892.3 6.0 convert_bitcast_fusion.2
  898.3 35.9 %reduce-scatter.33.cloned.1.call-done = bf16[256,1,1024]{2,0,1:T(8,128)(2,1)} async-done(((bf16[1024,1,1024]{2,0,1:T(8,128)(2,1)}), bf16[256,1,1024]{2,0,1:T(8,128)(2,1)}) %reduce-scatter.33.cloned.1.call-update) | async-done | bytes 524304 | tf_op jit(solution)/shard_map/reduce_scatter | solution.py:220
  936.4 42.8 %reduce-scatter.31.cloned.1.call-done = bf16[256,1,1024]{2,0,1:T(8,128)(2,1)} async-done(((bf16[1024,1,1024]{2,0,1:T(8,128)(2,1)}), bf16[256,1,1024]{2,0,1:T(8,128)(2,1)}) %reduce-scatter.31.cloned.1.call-update) | async-done | bytes 524304 | tf_op jit(solution)/shard_map/reduce_scatter | solution.py:208
  986.4 40.6 %all-gather.33.cloned.1.call-done = bf16[1024,1,1024]{2,0,1:T(8,128)(2,1)} async-done(((bf16[256,1,1024]{2,0,1:T(8,128)(2,1)}), bf16[1024,1,1024]{2,0,1:T(8,128)(2,1)}) %all-gather.33.cloned.1.call-update) | async-done | bytes 2097168 | tf_op jit(solution)/shard_map/all_gather | solution.py:201
  1033.1 111.2 %while.111 = (s32[]{:T(128)}, f32[4,1024,64]{1,2,0:T(8,128)}, f32[4,1024,64]{1,2,0:T(8,128)}, bf16[4,1024,64]{1,2,0:T(8,128)(2,1)}, bf16[4,1024,64]{2,1,0:T(8,12...) while((s32[]{:T(128)}, f32[4,1024,64]{1,2,0:T(8,128)}, ...), condition=%wide.region_31.32_spmd, body=%wide.region_27.31_spmd.sunk | while | flops 340098560 | bytes 21657452 | solution.py:158
  1039.9 17.1 while.116
  1067.7 17.1 while.116
  1095.5 17.1 while.116
  1123.3 17.1 while.116
  1158.2 42.9 %reduce-scatter.35.cloned.1.call-done = bf16[256,1,1024]{2,0,1:T(8,128)(2,1)} async-done(((bf16[1024,1,1024]{2,0,1:T(8,128)(2,1)}), bf16[256,1,1024]{2,0,1:T(8,128)(2,1)}) %reduce-scatter.35.cloned.1.call-update) | async-done | bytes 524304 | tf_op jit(solution)/shard_map/reduce_scatter | solution.py:220
  1207.0 43.5 %all-gather.35.cloned.1.call-done = bf16[1024,1,1024]{2,0,1:T(8,128)(2,1)} async-done(((bf16[256,1,1024]{2,0,1:T(8,128)(2,1)}), bf16[1024,1,1024]{2,0,1:T(8,128)(2,1)}) %all-gather.35.cloned.1.call-update) | async-done | bytes 2097168 | tf_op jit(solution)/shard_map/all_gather | solution.py:201
  1250.5 7.2 convert_reduce_fusion.1
  1263.0 42.9 %reduce-scatter.37.cloned.1.call-done = bf16[256,1,1024]{2,0,1:T(8,128)(2,1)} async-done(((bf16[1024,1,1024]{2,0,1:T(8,128)(2,1)}), bf16[256,1,1024]{2,0,1:T(8,128)(2,1)}) %reduce-scatter.37.cloned.1.call-update) | async-done | bytes 524304 | tf_op jit(solution)/shard_map/reduce_scatter | solution.py:220
  1329.8 5.9 fusion.131
  1335.8 6.0 fusion.124
  1346.8 8.7 all-gather.37.cloned.1.call-done
  1361.4 111.2 %while.113 = (s32[]{:T(128)}, f32[4,1024,64]{1,2,0:T(8,128)}, f32[4,1024,64]{1,2,0:T(8,128)}, bf16[4,1024,64]{1,2,0:T(8,128)(2,1)}, bf16[4,1024,64]{2,1,0:T(8,12...) while((s32[]{:T(128)}, f32[4,1024,64]{1,2,0:T(8,128)}, ...), condition=%wide.region_42.43_spmd, body=%wide.region_38.42_spmd.sunk | while | flops 340098560 | bytes 21657452 | solution.py:158
  1368.2 17.1 while.117
  1396.0 17.1 while.117
  1423.8 17.1 while.117
  1451.6 17.1 while.117
  1499.7 68.6 %collective-permute-done.9 = f32[256,1,1024]{2,0,1:T(8,128)} collective-permute-done((f32[256,1,1024]{2,0,1:T(8,128)}, f32[256,1,1024]{2,0,1:T(8,128)}, u32[]{:S(2)}, u32[]{:S(2)}) %collective-permute-start.9) | collective-permute-done | bytes 1048608 | tf_op jit(solution)/shard_map/ppermute | solution.py:19
  1572.9 27.0 %reduce-scatter.53.cloned.1.call-done = bf16[128,1024]{1,0:T(8,128)(2,1)} async-done(((bf16[1024,1024]{1,0:T(8,128)(2,1)}), bf16[128,1024]{1,0:T(8,128)(2,1)}) %reduce-scatter.53.cloned.1.call-update) | async-done | bytes 262160
  1604.0 105.2 %reduce-scatter.47.cloned.1.call-done = bf16[128,1024]{1,0:T(8,128)(2,1)} async-done(((bf16[1024,1024]{1,0:T(8,128)(2,1)}), bf16[128,1024]{1,0:T(8,128)(2,1)}) %reduce-scatter.47.cloned.1.call-update) | async-done | bytes 262160 | tf_op jit(solution)/shard_map/reduce_scatter | solution.py:362
  1709.3 90.9 %reduce-scatter.45.cloned.1.call-done = bf16[128,1024]{1,0:T(8,128)(2,1)} async-done(((bf16[1024,1024]{1,0:T(8,128)(2,1)}), bf16[128,1024]{1,0:T(8,128)(2,1)}) %reduce-scatter.45.cloned.1.call-update) | async-done | bytes 262160 | tf_op jit(solution)/shard_map/reduce_scatter | solution.py:362
  1809.9 79.9 %reduce-scatter.43.cloned.1.call-done = bf16[128,3,256]{2,0,1:T(8,128)(2,1)} async-done(((bf16[1024,3,256]{2,0,1:T(8,128)(2,1)}), bf16[128,3,256]{2,0,1:T(8,128)(2,1)}) %reduce-scatter.43.cloned.1.call-update) | async-done | bytes 196624 | tf_op jit(solution)/shard_map/reduce_scatter | solution.py:360
  1889.8 71.2 %reduce-scatter.41.cloned.1.call-done = bf16[128,3,256]{2,0,1:T(8,128)(2,1)} async-done(((bf16[1024,3,256]{2,0,1:T(8,128)(2,1)}), bf16[128,3,256]{2,0,1:T(8,128)(2,1)}) %reduce-scatter.41.cloned.1.call-update) | async-done | bytes 196624 | tf_op jit(solution)/shard_map/reduce_scatter | solution.py:360
  1966.6 48.2 %reduce-scatter.39.cloned.1.call-done = bf16[256,1,1024]{2,0,1:T(8,128)(2,1)} async-done(((bf16[1024,1,1024]{2,0,1:T(8,128)(2,1)}), bf16[256,1,1024]{2,0,1:T(8,128)(2,1)}) %reduce-scatter.39.cloned.1.call-update) | async-done | bytes 524304 | tf_op jit(solution)/shard_map/reduce_scatter | solution.py:220
  2021.2 45.7 %reduce-scatter.49.cloned.1.call-done = bf16[128,256]{1,0:T(8,128)(2,1)} async-done(((bf16[1024,256]{1,0:T(8,128)(2,1)}), bf16[128,256]{1,0:T(8,128)(2,1)}) %reduce-scatter.49.cloned.1.call-update) | async-done | bytes 65552
  2067.9 5.9 collective-permute-start.14
  2074.2 27.7 %all-reduce.1 = (f32[2,3,256]{2,1,0:T(4,128)S(1)}, f32[2,1024]{1,0:T(2,128)S(1)}) all-reduce(f32[2,3,256]{2,1,0:T(4,128)S(1)} %pad_maximum_fusion.9, f32[2,1024]{1,0:T(2,128)S(1)} %pad_maximum_fusion.10), channel_id=1, replica_groups=mesh['dh'=4,'b'=2,'th'=2,'tl'=2] {'dh','th'}, use_global_device_ids=true, to_apply=%region_50.51 | all-reduce | flops 3584 | bytes 28672 | tf_op jit(solution)/shard_map/psum | solution.py:373
  2101.9 9.9 collective-permute-start.16
  2118.3 36.9 %all-reduce = (f32[2,2,1024]{2,1,0:T(2,128)}, f32[2,2,1024]{2,1,0:T(2,128)}, f32[2,2,1024]{2,1,0:T(2,128)}) all-reduce(f32[2,2,1024]{2,1,0:T(2,128)S(1)} %pad_maximum_fusion.6, f32[2,2,1024]{2,1,0:T(2,128)S(1)} %pad_maximum_fusion.7, ...), channel_id=1, replica_groups=mesh['dh'=4,'b'=2,'th'=2,'tl'=2] {'dh','th','b','tl'}, use_global_device_ids=true, to_apply=%region_64.65 | all-reduce | flops 12288 | bytes 98304 | tf_op jit(solution)/shard_map/psum | solution.py:370
  (836 shorter events, 557.0 us)
Async XLA Ops:
  7.2 90.0 %all-gather.39.cloned.1.call-start = ((), (), s32[]{:S(2)}) async-start(), calls=%async_computation.36 | async-start | bytes 1769472 | tf_op jit(solution)/shard_map/all_gather | solution.py:231
  8.5 15.3 collective-permute-start.1
  24.6 118.3 %all-gather.23.cloned.1.call-start = ((), (), s32[]{:S(2)}) async-start(), calls=%async_computation.16 | async-start | bytes 2621440 | tf_op jit(solution)/shard_map/all_gather | solution.py:198
  24.6 17.3 collective-permute-start
  41.9 423.0 %copy-start = (bf16[256,1,1024]{2,0,1:T(8,128)(2,1)}, bf16[256,1,1024]{2,0,1:T(8,128)(2,1)S(1)}, u32[]{:S(2)}) copy-start(bf16[256,1,1024]{2,0,1:T(8,128)(2,1)S(1)} %collective-permute-done) | copy-start | bytes 1572868
  44.0 204.0 %reduce-scatter.25.cloned.1.call-start = ((), (), s32[]{:S(2)}) async-start(), calls=%async_computation.17 | async-start | bytes 2621440 | tf_op jit(solution)/shard_map/reduce_scatter | solution.py:208
  44.1 8.6 collective-permute-start.2
  46.0 7.3 collective-permute-start.3
  50.6 8.0 collective-permute-start.4
  54.2 524.2 %copy-start.12 = (f32[1024,10]{0,1:T(8,128)}, f32[1024,10]{0,1:T(8,128)S(1)}, u32[]{:S(2)}) copy-start(f32[1024,10]{0,1:T(8,128)S(1)} %get-tuple-element.846) | copy-start | bytes 122884
  54.2 524.2 %copy-start.15 = (f32[1024,10]{0,1:T(8,128)}, f32[1024,10]{0,1:T(8,128)S(1)}, u32[]{:S(2)}) copy-start(f32[1024,10]{0,1:T(8,128)S(1)} %get-tuple-element.847) | copy-start | bytes 122884
  199.6 107.1 %all-gather.41.cloned.1.call-start = ((), (), s32[]{:S(2)}) async-start(), calls=%async_computation.37 | async-start | bytes 2359296 | tf_op jit(solution)/shard_map/all_gather | solution.py:233
  199.6 20.2 collective-permute-start.5
  220.7 130.9 %all-gather.25.cloned.1.call-start = ((), (), s32[]{:S(2)}) async-start(), calls=%async_computation.18 | async-start | bytes 2621440 | tf_op jit(solution)/shard_map/all_gather | solution.py:198
  221.4 243.5 %copy-start.48 = (f32[1,1,1024]{2,1,0:T(1,128)}, f32[1,1,1024]{2,1,0:T(1,128)S(1)}, u32[]{:S(2)}) copy-start(f32[1,1,1024]{2,1,0:T(1,128)S(1)} %get-tuple-element.841) | copy-start | bytes 12292
  249.3 116.5 %copy-start.63 = (f32[256]{0:T(256)}, f32[256]{0:T(256)S(1)}, u32[]{:S(2)}) copy-start(f32[256]{0:T(256)S(1)} %broadcast_multiply_fusion.10) | copy-start | bytes 3076
  252.9 164.6 %all-gather.43.cloned.1.call-start = ((), (), s32[]{:S(2)}) async-start(), calls=%async_computation.38 | async-start | bytes 2359296 | tf_op jit(solution)/shard_map/all_gather | solution.py:234
  253.0 19.9 collective-permute-start.7
  273.7 191.1 %reduce-scatter.27.cloned.1.call-start = ((), (), s32[]{:S(2)}) async-start(), calls=%async_computation.19 | async-start | bytes 2621440 | tf_op jit(solution)/shard_map/reduce_scatter | solution.py:208
  273.8 7.5 collective-permute-start.6
  422.9 105.9 %all-gather.45.cloned.1.call-start = ((), (), s32[]{:S(2)}) async-start(), calls=%async_computation.39 | async-start | bytes 1769472 | tf_op jit(solution)/shard_map/all_gather | solution.py:231
  423.7 149.6 %all-gather.27.cloned.1.call-start = ((), (), s32[]{:S(2)}) async-start(), calls=%async_computation.20 | async-start | bytes 2621440 | tf_op jit(solution)/shard_map/all_gather | solution.py:198
  468.3 196.7 %reduce-scatter.29.cloned.1.call-start = ((), (), s32[]{:S(2)}) async-start(), calls=%async_computation.21 | async-start | bytes 2621440 | tf_op jit(solution)/shard_map/reduce_scatter | solution.py:208
  622.1 101.9 %all-gather.47.cloned.1.call-start = ((), (), s32[]{:S(2)}) async-start(), calls=%async_computation.40 | async-start | bytes 2359296 | tf_op jit(solution)/shard_map/all_gather | solution.py:233
  622.8 145.6 %all-gather.29.cloned.1.call-start = ((), (), s32[]{:S(2)}) async-start(), calls=%async_computation.22 | async-start | bytes 2621440 | tf_op jit(solution)/shard_map/all_gather | solution.py:198
  667.7 146.3 %all-gather.31.cloned.1.call-start = ((), (), s32[]{:S(2)}) async-start(), calls=%async_computation.24 | async-start | bytes 2621440 | tf_op jit(solution)/shard_map/all_gather | solution.py:201
  667.7 21.3 collective-permute-start.10
  672.3 16.1 collective-permute-start.8
  690.6 189.3 %all-gather.49.cloned.1.call-start = ((), (), s32[]{:S(2)}) async-start(), calls=%async_computation.41 | async-start | bytes 2359296 | tf_op jit(solution)/shard_map/all_gather | solution.py:234
  691.2 243.1 %reduce-scatter.33.cloned.1.call-start = ((), (), s32[]{:S(2)}) async-start(), calls=%async_computation.25 | async-start | bytes 2621440 | tf_op jit(solution)/shard_map/reduce_scatter | solution.py:220
  892.2 86.9 %reduce-scatter.31.cloned.1.call-start = ((), (), s32[]{:S(2)}) async-start(), calls=%async_computation.23 | async-start | bytes 2621440 | tf_op jit(solution)/shard_map/reduce_scatter | solution.py:208
  898.3 128.8 %all-gather.33.cloned.1.call-start = ((), (), s32[]{:S(2)}) async-start(), calls=%async_computation.26 | async-start | bytes 2621440 | tf_op jit(solution)/shard_map/all_gather | solution.py:201
  983.1 218.0 %reduce-scatter.35.cloned.1.call-start = ((), (), s32[]{:S(2)}) async-start(), calls=%async_computation.27 | async-start | bytes 2621440 | tf_op jit(solution)/shard_map/reduce_scatter | solution.py:220
  1158.1 92.3 %all-gather.35.cloned.1.call-start = ((), (), s32[]{:S(2)}) async-start(), calls=%async_computation.28 | async-start | bytes 2621440 | tf_op jit(solution)/shard_map/all_gather | solution.py:201
  1206.5 99.4 %reduce-scatter.37.cloned.1.call-start = ((), (), s32[]{:S(2)}) async-start(), calls=%async_computation.29 | async-start | bytes 2621440 | tf_op jit(solution)/shard_map/reduce_scatter | solution.py:220
  1262.9 92.6 %all-gather.37.cloned.1.call-start = ((), (), s32[]{:S(2)}) async-start(), calls=%async_computation.30 | async-start | bytes 2621440 | tf_op jit(solution)/shard_map/all_gather | solution.py:201
  1311.5 187.0 %reduce-scatter.55.cloned.1.call-start = ((), (), s32[]{:S(2)}) async-start(), calls=%async_computation.45 | async-start | bytes 2359296
  1318.8 253.1 %reduce-scatter.51.cloned.1.call-start = ((), (), s32[]{:S(2)}) async-start(), calls=%async_computation.43 | async-start | bytes 589824
  1322.3 277.6 %reduce-scatter.53.cloned.1.call-start = ((), (), s32[]{:S(2)}) async-start(), calls=%async_computation.44 | async-start | bytes 2359296
  1329.6 379.7 %reduce-scatter.47.cloned.1.call-start = ((), (), s32[]{:S(2)}) async-start(), calls=%async_computation.35 | async-start | bytes 2359296 | tf_op jit(solution)/shard_map/reduce_scatter | solution.py:362
  1335.8 464.4 %reduce-scatter.45.cloned.1.call-start = ((), (), s32[]{:S(2)}) async-start(), calls=%async_computation.34 | async-start | bytes 2359296 | tf_op jit(solution)/shard_map/reduce_scatter | solution.py:362
  1341.9 548.0 %reduce-scatter.43.cloned.1.call-start = ((), (), s32[]{:S(2)}) async-start(), calls=%async_computation.33 | async-start | bytes 1769472 | tf_op jit(solution)/shard_map/reduce_scatter | solution.py:360
  1346.7 614.3 %reduce-scatter.41.cloned.1.call-start = ((), (), s32[]{:S(2)}) async-start(), calls=%async_computation.32 | async-start | bytes 1769472 | tf_op jit(solution)/shard_map/reduce_scatter | solution.py:360
  1489.1 525.7 %reduce-scatter.39.cloned.1.call-start = ((), (), s32[]{:S(2)}) async-start(), calls=%async_computation.31 | async-start | bytes 2621440 | tf_op jit(solution)/shard_map/reduce_scatter | solution.py:220
  1493.8 573.2 %reduce-scatter.49.cloned.1.call-start = ((), (), s32[]{:S(2)}) async-start(), calls=%async_computation.42 | async-start | bytes 589824
  1493.8 74.5 %collective-permute-start.9 = (f32[256,1,1024]{2,0,1:T(8,128)}, f32[256,1,1024]{2,0,1:T(8,128)}, u32[]{:S(2)}, u32[]{:S(2)}) collective-permute-start(f32[256,1,1024]{2,0,1:T(8,128)} %get-tuple-element.774), channel_id=1, source_target_pairs={{0,0},{2,4},{4,2},{6,6},{1,1},{3,5},{5,3},{7,7},{8,8},{10,12},{12,... | collective-permute-start | bytes 3145736 | tf_op jit(solution)/shard_map/ppermute | solution.py:19
  1602.1 499.8 %collective-permute-start.17 = (f32[2,1024,128]{2,1,0:T(8,128)}, f32[2,1024,128]{2,1,0:T(8,128)}, u32[]{:S(2)}, u32[]{:S(2)}) collective-permute-start(f32[2,1024,128]{2,1,0:T(8,128)} %maximum_convert_fusion.1), channel_id=1, source_target_pairs={{0,0},{2,4},{4,2},{6,6},{1,1},{3,5},{5,3},{7,7},{8,8},{10,12},{12,... | collective-permute-start | bytes 3145736 | tf_op jit(solution)/shard_map/ppermute | solution.py:19
  1802.3 212.5 %copy-start.2 = (bf16[256,1,1024]{2,0,1:T(8,128)(2,1)S(1)}, bf16[256,1,1024]{2,0,1:T(8,128)(2,1)}, u32[]{:S(2)}) copy-start(bf16[256,1,1024]{2,0,1:T(8,128)(2,1)} %copy-done) | copy-start | bytes 1572868
  1802.3 212.5 %copy-start.53 = (f32[1,1,1024]{2,1,0:T(1,128)S(1)}, f32[1,1,1024]{2,1,0:T(1,128)}, u32[]{:S(2)}) copy-start(f32[1,1,1024]{2,1,0:T(1,128)} %copy-done.52) | copy-start | bytes 12292
  1802.3 212.5 %copy-start.62 = (f32[256]{0:T(256)S(1)}, f32[256]{0:T(256)}, u32[]{:S(2)}) copy-start(f32[256]{0:T(256)} %copy-done.61) | copy-start | bytes 3076
  1802.3 212.5 %copy-start.80 = (f32[256]{0:T(256)S(1)}, f32[256]{0:T(256)}, u32[]{:S(2)}) copy-start(f32[256]{0:T(256)} %copy-done.79) | copy-start | bytes 3076
  1802.3 214.2 %copy-start.27 = (f32[256,1,1024]{2,0,1:T(8,128)S(1)}, f32[256,1,1024]{2,0,1:T(8,128)}, u32[]{:S(2)}) copy-start(f32[256,1,1024]{2,0,1:T(8,128)} %get-tuple-element.675) | copy-start | bytes 3145732
  1802.3 309.5 %collective-permute-start.15 = (f32[2,128,1024]{2,1,0:T(8,128)}, f32[2,128,1024]{2,1,0:T(8,128)}, u32[]{:S(2)}, u32[]{:S(2)}) collective-permute-start(f32[2,128,1024]{2,1,0:T(8,128)} %maximum_convert_fusion), channel_id=1, source_target_pairs={{0,0},{2,4},{4,2},{6,6},{1,1},{3,5},{5,3},{7,7},{8,8},{10,12},{12,... | collective-permute-start | bytes 3145736 | tf_op jit(solution)/shard_map/ppermute | solution.py:19
  1809.9 211.3 %copy-start.88 = (f32[1024]{0:T(1024)S(1)}, f32[1024]{0:T(1024)}, u32[]{:S(2)}) copy-start(f32[1024]{0:T(1024)} %get-tuple-element.836) | copy-start | bytes 12292
  1809.9 211.3 %copy-start.91 = (f32[1024]{0:T(1024)S(1)}, f32[1024]{0:T(1024)}, u32[]{:S(2)}) copy-start(f32[1024]{0:T(1024)} %get-tuple-element.838) | copy-start | bytes 12292
  1809.9 211.3 %copy-start.72 = (f32[1024]{0:T(1024)S(1)}, f32[1024]{0:T(1024)}, u32[]{:S(2)}) copy-start(f32[1024]{0:T(1024)} %get-tuple-element.676) | copy-start | bytes 12292
  1809.9 211.3 %copy-start.82 = (f32[1024]{0:T(1024)S(1)}, f32[1024]{0:T(1024)}, u32[]{:S(2)}) copy-start(f32[1024]{0:T(1024)} %get-tuple-element.673) | copy-start | bytes 12292
  1962.9 155.3 %copy-start.71 = (f32[1024]{0:T(1024)S(1)}, f32[1024]{0:T(1024)}, u32[]{:S(2)}) copy-start(f32[1024]{0:T(1024)} %get-tuple-element.545) | copy-start | bytes 12292
  1963.0 155.3 %copy-start.70 = (f32[1024]{0:T(1024)S(1)}, f32[1024]{0:T(1024)}, u32[]{:S(2)}) copy-start(f32[1024]{0:T(1024)} %get-tuple-element.532) | copy-start | bytes 12292
  1963.0 155.3 %collective-permute-start.12 = (f32[2,128,3,256]{3,1,2,0:T(8,128)}, f32[2,128,3,256]{3,1,2,0:T(8,128)}, u32[]{:S(2)}, u32[]{:S(2)}) collective-permute-start(f32[2,128,3,256]{3,1,2,0:T(8,128)} %maximum_convert_fusion.2), channel_id=1, source_target_pairs={{0,0},{2,4},{4,2},{6,6},{1,1},{3,5},{5,3},{7,7},{8,8},{10,12},{12,... | collective-permute-start | bytes 2359304 | tf_op jit(solution)/shard_map/ppermute | solution.py:19
  2018.9 136.3 %collective-permute-start.11 = (f32[256,1,1024]{2,0,1:T(8,128)}, f32[256,1,1024]{2,0,1:T(8,128)S(1)}, u32[]{:S(2)}, u32[]{:S(2)}) collective-permute-start(f32[256,1,1024]{2,0,1:T(8,128)} %fusion.194), channel_id=1, source_target_pairs={{0,0},{2,4},{4,2},{6,6},{1,1},{3,5},{5,3},{7,7},{8,8},{10,12},{12,... | collective-permute-start | bytes 3145736 | tf_op jit(solution)/shard_map/ppermute | solution.py:19
  2067.9 50.3 %collective-permute-start.14 = (f32[2,256,128]{2,1,0:T(8,128)S(1)}, f32[2,256,128]{2,1,0:T(8,128)S(1)}, u32[]{:S(2)}, u32[]{:S(2)}) collective-permute-start(f32[2,256,128]{2,1,0:T(8,128)S(1)} %maximum_convert_fusion.3), channel_id=1, source_target_pairs={{0,0},{2,4},{4,2},{6,6},{1,1},{3,5},{5,3},{7,7},{8,8},{10,12},{12,... | collective-permute-start | bytes 786440 | tf_op jit(solution)/shard_map/ppermute | solution.py:19
  2101.9 16.3 collective-permute-start.16
  2111.8 5.9 collective-permute-start.13
  (91 other events, 3489.9 us)
Sparse Core Ops, SparseCore 0:
  24.7 71.5 all-gather.38
  98.4 44.3 all-gather.22
  199.7 48.3 reduce-scatter.24
  250.4 56.2 all-gather.40
  308.7 42.8 all-gather.24
  353.8 63.6 all-gather.42
  423.0 41.8 reduce-scatter.26
  467.0 61.7 all-gather.44
  530.4 42.8 all-gather.26
  622.2 42.8 reduce-scatter.28
  668.1 55.8 all-gather.46
  725.5 42.8 all-gather.28
  770.0 43.8 all-gather.30
  816.2 63.6 all-gather.48
  892.4 41.8 reduce-scatter.32
  936.4 42.7 reduce-scatter.30
  983.2 43.8 all-gather.32
  1158.2 42.7 reduce-scatter.34
  1206.6 43.8 all-gather.34
  1263.1 42.8 reduce-scatter.36
  1311.7 43.8 all-gather.36
  1357.9 89.6 reduce-scatter.54
  1450.0 31.6 reduce-scatter.50
  1483.8 116.1 reduce-scatter.52
  1602.2 106.9 reduce-scatter.46
  1711.4 88.7 reduce-scatter.44
  1802.3 87.4 reduce-scatter.42
  1892.1 68.8 reduce-scatter.40
  1963.3 51.4 reduce-scatter.38
  2017.0 49.9 reduce-scatter.48
